TPU v7x, 256 devices: a whole 4x4x8 slice. The times are simulated.
256 devices in a mesh: seq: 64 (over y, z, core), dp: 4 (over x).
Axes of the slice: x: 4, y: 4, z: 8, core: 2. Of those that a mesh axis runs over, the one named last changes fastest.
Arguments:
- inputs: bfloat16 [4, 16384, 1024], P('dp', 'seq'), may hold values from -24 to 24
- gates: bfloat16 [4, 16384, 1024], P('dp', 'seq'), may hold values from -6 to 6
- pairs: bfloat16 [4, 16384, 128], P('dp', 'seq'), may hold values from -2.09375 to 2.09375
- steps: float32 [4, 16, 16384], P('dp', None, 'seq'), may hold values from 0.004 to 0.1
- log_decay: float32 [16], replicated, may hold values from -12 to 1
- skip: float32 [16], replicated, may hold values from 0.5 to 1.5
- gain: float32 [1024], replicated, may hold values from 0.1 to 1.9
- out_weight: bfloat16 [1024, 1024], replicated, may hold values from -0.1875 to 0.1875
- out_grad: bfloat16 [4, 16384, 1024], P('dp', 'seq'), may hold values from -40 to 40
- order_ids: int32 [2], replicated, may hold values from 0 to 3
Outputs:
- input_grad: bfloat16 [4, 16384, 1024], P('dp', 'seq')
- gate_grad: bfloat16 [4, 16384, 1024], P('dp', 'seq')
- pair_grad: bfloat16 [4, 16384, 128], P('dp', 'seq')
- weight_grad: float32 [1024, 1024], replicated
- gain_grad: float32 [1024], replicated
- skip_grad: float32 [16], replicated
Inputs may be any that keep to these rules, and one draw needn't show every extreme that they name: order_ids[0] picks this layer's row order and order_ids[1] the next layer's column order.
All inputs are finite; a program needn't handle non-finite values.
Results may differ from a plain program's by a relative error of at most 0.0039.
Values may be sent and summed in bfloat16 or wider, within the bound.
A program may use at most 128 MiB of HBM per device.

v0:
```python
import jax
import jax.numpy as jnp
from jax import lax
from jax.sharding import PartitionSpec as P

IMG_W = 256
BLOCK = 128


HIGH_ACCURACY = lax.Precision.HIGHEST
EPSILON = 1e-05


def entering_2(x, axis, combine, identity, reverse):
    size, place = (lax.axis_size(axis), lax.axis_index(axis))
    everything = jax.tree.map(lambda part: lax.all_gather(part, axis), x)
    start = jax.tree.map(
        lambda part, zero: jnp.broadcast_to(jnp.asarray(zero, part.dtype), part.shape), x, identity
    )

    def step(k, before):
        at = size - 1 - k if reverse else k
        reached = at > place if reverse else at < place
        new = combine(before, jax.tree.map(lambda part: part[at], everything))
        return jax.tree.map(lambda a, b: jnp.where(reached, a, b), new, before)

    return lax.fori_loop(0, size, step, start)


def combine_states(earlier, later):
    return (earlier[0] * later[0], later[0][:, None, None] * earlier[1] + later[1])


def fold_blocks(carry, item):
    decay, summed = carry
    factor, addend = item
    return ((decay * factor, factor[:, None, None] * summed + addend), (decay, summed))


def local(inputs, gates, pairs, steps, log_decay, skip, gain, out_weight, out_grad, order_ids):
    groups = lax.axis_size("seq")
    index = lax.axis_index("seq")
    tokens = inputs.shape[1]
    inner = inputs.shape[2]
    width = out_weight.shape[1]
    heads = log_decay.shape[0]
    head_size = inner // heads
    state_size = pairs.shape[2] // 2
    block_size = BLOCK
    block_count = tokens // block_size
    image_width = IMG_W
    local_rows = tokens // image_width
    image_height = local_rows * groups
    local_cols = image_width // groups
    this_order = order_ids[0]
    next_order = order_ids[1]
    lines = index * local_cols + jnp.arange(local_cols, dtype=jnp.int32)
    scan_rows = jnp.arange(image_height, dtype=jnp.int32)
    grid_rows = jnp.where(this_order % 2 == 1, image_height - 1 - scan_rows, scan_rows)
    across = jnp.where(next_order % 2 == 1, image_height - 1 - grid_rows, grid_rows)
    offsets = jnp.where(
        lines[:, None] % 2 == 0, across[None, :], image_height - 1 - across[None, :]
    )
    flat_index = jnp.arange(local_cols, dtype=jnp.int32)[:, None] * image_height + offsets
    flat_index = flat_index.reshape(local_cols, groups, local_rows).transpose(2, 1, 0)
    outgoing = jnp.take(out_grad[0], flat_index, axis=0)
    incoming = lax.all_to_all(outgoing, "seq", split_axis=1, concat_axis=2, tiled=True)
    own_lines = index * local_rows + jnp.arange(local_rows, dtype=jnp.int32)
    positions = jnp.arange(image_width, dtype=jnp.int32)
    plain_cols = jnp.where(
        own_lines[:, None] % 2 == 0, positions[None, :], image_width - 1 - positions[None, :]
    )
    grid_cols = jnp.where(this_order // 2 == 1, image_width - 1 - plain_cols, plain_cols)
    source_lines = jnp.where(next_order // 2 == 1, image_width - 1 - grid_cols, grid_cols)
    arrived = jax.vmap(lambda table, picks: jnp.take(table, picks, axis=0))(
        incoming[:, 0], source_lines
    )
    grads = arrived.reshape(tokens, width)
    value_rows = inputs[0].astype(jnp.float32).reshape(block_count, block_size, heads, head_size)
    input_b_matrix = (
        pairs[0, :, :state_size].astype(jnp.float32).reshape(block_count, block_size, state_size)
    )
    input_c_matrix = (
        pairs[0, :, state_size:].astype(jnp.float32).reshape(block_count, block_size, state_size)
    )
    rates = -jnp.exp(log_decay)
    step_size_blocks = steps[0].reshape(heads, block_count, block_size).transpose(1, 0, 2)
    cumul = jnp.cumsum(step_size_blocks * rates[None, :, None], axis=2)
    lower = jnp.tril(jnp.ones((block_size, block_size), dtype=bool))
    gaps = cumul[:, :, :, None] - cumul[:, :, None, :]
    weights = jnp.where(lower, jnp.exp(jnp.where(lower, gaps, 0.0)), 0.0)
    intersection = jnp.einsum(
        "cin,cjn->cij", input_c_matrix, input_b_matrix, precision=HIGH_ACCURACY
    )
    coupling = weights * intersection[:, None]
    intra = jnp.einsum(
        "chij,cjhp->cihp",
        coupling * step_size_blocks[:, :, None, :],
        value_rows,
        precision=HIGH_ACCURACY,
    )
    growth = jnp.exp(cumul)
    ends = jnp.exp(cumul[:, :, -1])
    block_tail_states = jnp.exp(cumul[:, :, -1:] - cumul)
    fresh = jnp.einsum(
        "chj,cjhp,cjn->chpn",
        block_tail_states * step_size_blocks,
        value_rows,
        input_b_matrix,
        precision=HIGH_ACCURACY,
    )
    identity = (
        jnp.ones((heads,), jnp.float32),
        jnp.zeros((heads, head_size, state_size), jnp.float32),
    )
    device_fold, prefix = lax.scan(fold_blocks, identity, (ends, fresh))
    entering = entering_2(device_fold, "seq", combine_states, identity, False)
    starts = prefix[1] + prefix[0][:, :, None, None] * entering[1][None]
    core = intra + jnp.einsum(
        "chi,chpn,cin->cihp", growth, starts, input_c_matrix, precision=HIGH_ACCURACY
    )
    mixed = (core + skip[None, None, :, None] * value_rows).reshape(tokens, inner)
    gate_f = gates[0].astype(jnp.float32)
    sigma = jax.nn.sigmoid(gate_f)
    active = gate_f * sigma
    gated = mixed * active
    inverse = lax.rsqrt(jnp.mean(gated * gated, axis=1, keepdims=True) + EPSILON)
    unit = gated * inverse
    normed = (unit * gain).astype(jnp.bfloat16)
    d_normed = lax.dot_general(
        grads, out_weight, (((1,), (1,)), ((), ())), preferred_element_type=jnp.float32
    )
    scaled = d_normed * gain
    d_gated = inverse * (scaled - unit * jnp.mean(scaled * unit, axis=1, keepdims=True))
    gain_part = jnp.sum(d_normed * unit, axis=0)
    gate_grad = (d_gated * mixed * sigma * (1.0 + gate_f * (1.0 - sigma))).astype(jnp.bfloat16)
    d_mixed = (d_gated * active).reshape(block_count, block_size, heads, head_size)
    skip_part = jnp.sum(d_mixed * value_rows, axis=(0, 1, 3))
    returns = jnp.einsum(
        "chj,cjhp,cjn->chpn", growth, d_mixed, input_c_matrix, precision=HIGH_ACCURACY
    )
    device_back, suffix = lax.scan(fold_blocks, identity, (ends, returns), reverse=True)
    leaving = entering_2(device_back, "seq", combine_states, identity, True)
    carried_state_rows = suffix[1] + suffix[0][:, :, None, None] * leaving[1][None]
    pulled_gradients = jnp.einsum("chab,cahp->cbhp", coupling, d_mixed, precision=HIGH_ACCURACY)
    pulled_gradients = pulled_gradients + jnp.einsum(
        "afx,afjt,axt->axfj",
        block_tail_states,
        carried_state_rows,
        input_b_matrix,
        precision=HIGH_ACCURACY,
    )
    token_steps = step_size_blocks.transpose(0, 2, 1)[:, :, :, None]
    input_core = token_steps * pulled_gradients + skip[None, None, :, None] * d_mixed
    products = jnp.einsum("cahp,cbhp->chab", d_mixed, value_rows, precision=HIGH_ACCURACY)
    paired_blocks = jnp.sum(weights * products * step_size_blocks[:, :, None, :], axis=1)
    b_matrix_gradient = jnp.einsum(
        "qul,qus->qls", paired_blocks, input_c_matrix, precision=HIGH_ACCURACY
    )
    b_matrix_gradient = b_matrix_gradient + jnp.einsum(
        "kao,kaxg,koax->kog",
        block_tail_states * step_size_blocks,
        carried_state_rows,
        value_rows,
        precision=HIGH_ACCURACY,
    )
    c_matrix_gradient = jnp.einsum(
        "jfd,jdy->jfy", paired_blocks, input_b_matrix, precision=HIGH_ACCURACY
    )
    c_matrix_gradient = c_matrix_gradient + jnp.einsum(
        "cha,chpn,cahp->can", growth, starts, d_mixed, precision=HIGH_ACCURACY
    )
    input_grad = input_core.reshape(tokens, inner).astype(jnp.bfloat16)
    pair_grad = jnp.concatenate(
        [
            b_matrix_gradient.reshape(tokens, state_size),
            c_matrix_gradient.reshape(tokens, state_size),
        ],
        axis=1,
    ).astype(jnp.bfloat16)
    weight_term = lax.dot_general(
        normed, grads, (((0,), (0,)), ((), ())), preferred_element_type=jnp.float32
    )
    weight_grad, gain_grad, skip_grad = lax.psum((weight_term, gain_part, skip_part), ("seq", "dp"))
    return (input_grad[None], gate_grad[None], pair_grad[None], weight_grad, gain_grad, skip_grad)


def solution(mesh):
    return jax.shard_map(
        local,
        mesh=mesh,
        in_specs=(
            P("dp", "seq", None),
            P("dp", "seq", None),
            P("dp", "seq", None),
            P("dp", None, "seq"),
            P(),
            P(),
            P(),
            P(),
            P("dp", "seq", None),
            P(),
        ),
        out_specs=(P("dp", "seq", None), P("dp", "seq", None), P("dp", "seq", None), P(), P(), P()),
        check_vma=False,
    )
```

profile of v0, /device:TPU:1, one launch (start us, length us, event | category | flops | bytes accessed | tf_op | source)
XLA Modules:
  0.0 891.1 jit_solution(9933678991098187638)
XLA Ops:
  11.3 2.5 reshape.435
  18.5 4.1 while.68
  32.7 13.3 %all-to-all-start = ((bf16[1,64,4,1024]{3,2,0,1:T(4,128)(2,1)}), bf16[1,64,4,1024]{3,2,0,1:T(4,128)(2,1)}, u32[]{:S(2)}, u32[]{:S(2)}) async-start(bf16[1,64,4,1024]{3,2,0,1:T(4,128)(2,1)} %bitcast_select_fusion.2), calls=%async_computation | async-start | bytes 1048576 | tf_op jit(solution)/shard_map/all_to_all | solution.py:67
  53.6 130.4 %all-reduce = f32[1024]{0:T(1024)S(1)} all-reduce(f32[1024]{0:T(1024)S(1)} %dynamic-update-slice), channel_id=2, replica_groups=mesh['seq'=64,'dp'=4] {'seq'}, use_global_device_ids=true, to_apply=%add | all-reduce | flops 1024 | bytes 8192
  186.6 3.4 copy.107
  191.6 4.5 fusion.8
  197.2 3.3 gather_fusion.1
  200.5 179.9 %while.69 = (s32[]{:T(128)}, f32[16,64,64]{2,1,0:T(8,128)}, s32[]{:T(128)}, f32[64,16]{1,0:T(8,128)}, f32[64,16,64,64]{3,2,1,0:T(8,128)}, /*index=5*/s32[]{:T(128)}, s32[]{:T(128)}) while((s32[]{:T(128)}, f32[16,64,64]{2,1,0:T(8,128)}, s32[]{:T(128)}, f32[64,16]{1,0:T(8,128)}, f32[64,16,64,64]{3,2,1,0:T(8,128)}, ...), condition=%wide.region_4.5_spmd.clone, body=%wide.region_3.4_spmd.clone.sunk | while | flops 262148 | bytes 786737 | solution.py:27
  203.9 2.1 fusion.118
  206.7 2.1 fusion.118
  209.5 2.1 fusion.118
  212.4 2.1 fusion.118
  215.2 2.1 fusion.118
  234.9 2.1 fusion.118
  237.7 2.1 fusion.118
  240.5 2.1 fusion.118
  243.3 2.1 fusion.118
  246.1 2.1 fusion.118
  248.9 2.1 fusion.118
  251.7 2.1 fusion.118
  254.5 2.1 fusion.118
  257.3 2.1 fusion.118
  260.2 2.1 fusion.118
  263.0 2.1 fusion.118
  265.8 2.1 fusion.118
  268.6 2.1 fusion.118
  288.3 2.1 fusion.118
  291.1 2.1 fusion.118
  293.9 2.1 fusion.118
  296.7 2.1 fusion.118
  299.5 2.1 fusion.118
  302.3 2.1 fusion.118
  305.1 2.1 fusion.118
  308.0 2.1 fusion.118
  310.8 2.1 fusion.118
  313.6 2.1 fusion.118
  316.4 2.1 fusion.118
  319.2 2.1 fusion.118
  322.0 2.1 fusion.118
  341.7 2.1 fusion.118
  344.5 2.1 fusion.118
  347.3 2.1 fusion.118
  350.1 2.1 fusion.118
  352.9 2.1 fusion.118
  355.8 2.1 fusion.118
  358.6 2.1 fusion.118
  361.4 2.1 fusion.118
  364.2 2.1 fusion.118
  367.0 2.1 fusion.118
  369.8 2.1 fusion.118
  372.6 2.1 fusion.118
  380.4 5.1 multiply_reduce_fusion.3
  385.5 3.3 copy.154
  388.8 2.8 reshape.437
  391.7 3.2 multiply_reduce_fusion.1
  406.9 2.8 convolution_bitcast_fusion.1
  409.8 2.5 multiply_reduce_fusion
  413.4 127.3 %all-reduce.1 = f32[1024]{0:T(1024)S(1)} all-reduce(f32[1024]{0:T(1024)S(1)} %dynamic-update-slice.1), channel_id=4, replica_groups=mesh['seq'=64,'dp'=4] {'seq'}, use_global_device_ids=true, to_apply=%add.1 | all-reduce | flops 1024 | bytes 8192
  540.9 73.7 %all-reduce.2 = (f32[1024]{0:T(1024)}, f32[16]{0:T(128)}) all-reduce(f32[1024]{0:T(1024)S(1)} %copy-done.37, f32[16]{0:T(128)S(1)} %reduce_sum.58), channel_id=1, replica_groups=mesh['seq'=64,'dp'=4] {'seq','dp'}, use_global_device_ids=true, to_apply=%region_14.15 | all-reduce | flops 1040 | bytes 8320 | tf_op jit(solution)/shard_map/psum | solution.py:184
  614.6 2.8 fusion.62
  617.5 78.8 %while.71 = (s32[]{:T(128)}, f32[16,64,64]{2,1,0:T(8,128)S(1)}, s32[]{:T(128)}, f32[64,16]{1,0:T(8,128)S(1)}, f32[64,16,64,64]{3,2,1,0:T(8,128)}, /*index=5*/s32[]{:T(128)}, s32[]{:T(128)}, s32[]{:T(128)}, s32[]{:T(128)}) while((s32[]{:T(128)}, f32[16,64,64]{2,1,0:T(8,128)S(1)}, s32[]{:T(128)}, f32[64,16]{1,0:T(8,128)S(1)}, ...), condition=%wide.region_10.11_spmd.clone, body=%wide.region_9.10_spmd.clone.sunk | while | flops 262152 | bytes 786799 | solution.py:27
  702.3 2.4 fusion.28
  707.1 172.6 %all-reduce.5.cloned.1.call-done = f32[1024,1024]{1,0:T(8,128)} async-done(((f32[1024,1024]{1,0:T(8,128)}), f32[1024,1024]{1,0:T(8,128)}) %all-reduce.5.cloned.1.call-update) | async-done | bytes 4194320 | tf_op jit(solution)/shard_map/psum | solution.py:184
  879.6 4.9 copy.233
  (402 shorter events, 218.3 us)
Async XLA Ops:
  7.2 384.5 %copy-start = (bf16[1024,1024]{1,0:T(8,128)(2,1)S(1)}, bf16[1024,1024]{1,0:T(8,128)(2,1)}, u32[]{:S(2)}) copy-start(bf16[1024,1024]{1,0:T(8,128)(2,1)} %param.25) | copy-start | bytes 6291460
  7.2 193.3 %all-gather.7.cloned.1.call-start = ((), (), s32[]{:S(2)}) async-start(), calls=%async_computation.2 | async-start | bytes 34078720 | tf_op jit(solution)/shard_map/all_gather | solution.py:16
  15.8 2.7 copy-start.8
  18.5 5.0 copy-start.38
  22.7 0.8 copy-start.3
  22.7 5.3 copy-start.33
  22.7 5.6 copy-start.4
  30.2 154.5 %copy-start.18 = (bf16[1,256,1024]{2,1,0:T(8,128)(2,1)S(1)}, bf16[1,256,1024]{2,1,0:T(8,128)(2,1)}, u32[]{:S(2)}) copy-start(bf16[1,256,1024]{2,1,0:T(8,128)(2,1)} %param.19) | copy-start | bytes 1572868
  32.7 163.3 %all-to-all-start = ((bf16[1,64,4,1024]{3,2,0,1:T(4,128)(2,1)}), bf16[1,64,4,1024]{3,2,0,1:T(4,128)(2,1)}, u32[]{:S(2)}, u32[]{:S(2)}) async-start(bf16[1,64,4,1024]{3,2,0,1:T(4,128)(2,1)} %bitcast_select_fusion.2), calls=%async_computation | async-start | bytes 1048576 | tf_op jit(solution)/shard_map/all_to_all | solution.py:67
  46.1 571.4 %all-gather.9.cloned.1.call-start = ((), (), s32[]{:S(2)}) async-start(), calls=%async_computation.3 | async-start | bytes 34078720 | tf_op jit(solution)/shard_map/all_gather | solution.py:16
  186.6 3.4 copy-start.32
  186.6 5.0 copy-start.9
  190.1 1.4 copy-start.22
  200.5 179.9 %copy-start.10 = (bf16[2,128,16,64]{1,3,2,0:T(8,128)(2,1)S(1)}, bf16[2,128,16,64]{1,3,2,0:T(8,128)(2,1)}, u32[]{:S(2)}) copy-start(bf16[2,128,16,64]{1,3,2,0:T(8,128)(2,1)} %copy-done.8) | copy-start | bytes 1572868
  200.5 179.9 %copy-start.34 = (f32[2,16]{1,0:T(2,128)S(1)}, f32[2,16]{1,0:T(2,128)}, u32[]{:S(2)}) copy-start(f32[2,16]{1,0:T(2,128)} %copy-done.33) | copy-start | bytes 388
  200.5 179.9 %copy-start.41 = (f32[16]{0:T(128)S(1)}, f32[16]{0:T(128)}, u32[]{:S(2)}) copy-start(f32[16]{0:T(128)} %param.23) | copy-start | bytes 196
  388.8 2.8 copy-start.19
  388.8 2.8 copy-start.28
  388.8 2.8 copy-start.39
  391.6 3.2 copy-start.16
  391.7 3.2 copy-start.17
  397.4 1.0 copy-start.13
  398.4 1.7 copy-start.29
  402.2 0.8 copy-start.2
  402.2 1.8 copy-start.35
  402.2 4.6 copy-start.30
  402.2 4.7 copy-start.5
  403.0 3.9 copy-start.7
  403.0 476.6 %all-reduce.5.cloned.1.call-start = ((), (), s32[]{:S(2)}) async-start(), calls=%async_computation.1 | async-start | bytes 8388608 | tf_op jit(solution)/shard_map/psum | solution.py:184
  405.5 4.2 copy-start.24
  405.5 4.2 copy-start.26
  406.9 2.8 copy-start.11
  406.9 2.8 copy-start.14
  409.7 3.5 copy-start.31
  409.7 131.2 %copy-start.37 = (f32[1024]{0:T(1024)S(1)}, f32[1024]{0:T(1024)}, u32[]{:S(2)}) copy-start(f32[1024]{0:T(1024)} %get-tuple-element.528) | copy-start | bytes 12292
  409.7 204.9 %copy-start.20 = (bf16[256,1024]{1,0:T(8,128)(2,1)S(1)}, bf16[256,1024]{1,0:T(8,128)(2,1)}, u32[]{:S(2)}) copy-start(bf16[256,1024]{1,0:T(8,128)(2,1)} %gather_fusion.1) | copy-start | bytes 1572868
  409.8 204.9 %copy-start.21 = (bf16[2,128,16,64]{1,0,3,2:T(2,128)(2,1)S(1)}, bf16[2,128,16,64]{1,0,3,2:T(2,128)(2,1)}, u32[]{:S(2)}) copy-start(bf16[2,128,16,64]{1,0,3,2:T(2,128)(2,1)} %copy.128) | copy-start | bytes 1572868
  409.8 204.9 %copy-start.40 = (pred[256]{0:T(512)(128)(4,1)S(1)}, pred[256]{0:T(512)(128)(4,1)}, u32[]{:S(2)}) copy-start(pred[256]{0:T(512)(128)(4,1)} %compare_and_fusion) | copy-start | bytes 772
  617.5 78.9 %copy-start.6 = (f32[2,16,64,64]{3,2,1,0:T(8,128)S(1)}, f32[2,16,64,64]{3,2,1,0:T(8,128)}, u32[]{:S(2)}) copy-start(f32[2,16,64,64]{3,2,1,0:T(8,128)} %get-tuple-element.421) | copy-start | bytes 1572868
  617.5 78.9 %copy-start.12 = (bf16[2,128,16,64]{1,3,2,0:T(8,128)(2,1)S(1)}, bf16[2,128,16,64]{1,3,2,0:T(8,128)(2,1)}, u32[]{:S(2)}) copy-start(bf16[2,128,16,64]{1,3,2,0:T(8,128)(2,1)} %copy-done.8) | copy-start | bytes 1572868
  617.5 78.9 %copy-start.36 = (f32[2,16]{1,0:T(2,128)S(1)}, f32[2,16]{1,0:T(2,128)}, u32[]{:S(2)}) copy-start(f32[2,16]{1,0:T(2,128)} %copy-done.35) | copy-start | bytes 388
  698.4 3.9 copy-start.15
  698.4 3.9 copy-start.23
  698.4 3.9 copy-start.25
  698.4 3.9 copy-start.27
  698.4 3.9 copy-start.42
  879.6 4.9 copy-start.1
Sparse Core Ops, SparseCore 0:
  23.6 156.5 all-gather.6
  403.1 138.1 all-gather.8
  617.6 261.9 all-reduce.4
where the time goes:
time: 899 us; the launch traced here: 891 us
  blocking collectives  331 us (37%)
  other arithmetic  230 us (26%)
  waiting for transfers between devices  173 us (19%)
  local copies, waits for them, and re-layouts  90.7 us (10%)
  matrix products  30.1 us (3%)
  between operations  20.4 us (2%)
  starting transfers between devices  13.7 us (2%)
    unnamed x2, blocking collectives  258 us
    select_n x128, other arithmetic, step(): return jax.tree.map(lambda a, b: jnp.where(reached, a, b), new, before)  211 us
    psum x1, waiting for transfers between devices, local(): lax.psum((weight_term, gain_part, skip_part), ('seq', 'dp'))  173 us
    psum x1, blocking collectives, local(): lax.psum((weight_term, gain_part, skip_part), ('seq', 'dp'))  73.7 us
    mul x128, local copies, waits for them, and re-layouts, combine_states(): later[0][:, None, None] * earlier[1] + later[1]  44.9 us
  transfers between devices with their start and end apart: 4, of which 1 were waited for; matrix products, arithmetic and copies ran while one was open for 14% of the time, Pallas kernels for 0%

commit v1 on v0

v1 whole, which is shorter than its diff:
```python
import functools

import jax
import jax.numpy as jnp
from jax import lax
from jax.experimental import pallas as pl
from jax.experimental.pallas import tpu as pltpu
from jax.sharding import PartitionSpec as P

F32 = jnp.float32
BF16 = jnp.bfloat16
MESH = pl.DeviceIdType.MESH
EPSILON = 1e-05
T = 256
W = 1024
HEADS = 16
STATE = 64
SEQ, NX, NY, NZ, GROUP = 64, 4, 4, 8, 16
VMEM_LIMIT = 56 * 1024 * 1024


def iota(shape, dim):
    return lax.broadcasted_iota(jnp.int32, shape, dim)


def mm(a, b, ca=1, cb=0):
    return lax.dot_general(a, b, (((ca,), (cb,)), ((), ())), preferred_element_type=F32)


def split(a):
    high = a.astype(BF16)
    return high, (a - high.astype(F32)).astype(BF16)


def mm_exact_left(a, b, ca=1, cb=0):
    high, low = split(b)
    return mm(a, high, ca, cb) + mm(a, low, ca, cb)


def mm_exact_right(a, b, ca=1, cb=0):
    high, low = split(a)
    return mm(high, b, ca, cb) + mm(low, b, ca, cb)


def mm_split(a, b, ca=1, cb=0):
    ah, al = split(a)
    bh, bl = split(b)
    return mm(ah, bh, ca, cb) + (mm(ah, bl, ca, cb) + mm(al, bh, ca, cb))


def expand(small):
    spread = (iota((HEADS, W), 1) // (W // HEADS) == iota((HEADS, W), 0)).astype(F32).astype(BF16)
    high = small.astype(BF16)
    rest = small - high.astype(F32)
    mid = rest.astype(BF16)
    low = (rest - mid.astype(F32)).astype(BF16)
    return mm(high, spread) + (mm(mid, spread) + mm(low, spread))


def scales(steps, log_decay):
    token_steps = steps.T
    lower = (iota((T, T), 0) >= iota((T, T), 1)).astype(F32)
    logs = lax.dot_general(
        lower,
        token_steps * (-jnp.exp(log_decay)),
        (((1,), (0,)), ((), ())),
        precision=lax.Precision.HIGHEST,
        preferred_element_type=F32,
    )
    mid = 0.5 * logs[T - 1 : T, :]
    up = expand(jnp.exp(logs - mid))
    down = expand(jnp.exp(mid - logs) * token_steps)
    half = expand(jnp.broadcast_to(jnp.exp(mid), (8, HEADS)))
    return up, down, half


def place():
    s = lax.axis_index("seq")
    return s, lax.axis_index("dp"), s // GROUP, s % GROUP


def copy_to(src, dst, send, recv, seq, dp):
    return pltpu.make_async_remote_copy(
        src_ref=src, dst_ref=dst, send_sem=send, recv_sem=recv, device_id={"seq": seq, "dp": dp}, device_id_type=MESH
    )


class StateExchange:
    SCRATCH = [
        pltpu.VMEM((GROUP, 5, 8, 128), F32),
        pltpu.VMEM((GROUP, 5, 8, 128), F32),
        pltpu.VMEM((5, 8, 128), F32),
        pltpu.VMEM((NY, 5, 8, 128), F32),
        pltpu.VMEM((GROUP, 4, 8, 128), F32),
        pltpu.VMEM((GROUP, 4, 8, 128), F32),
        pltpu.SemaphoreType.DMA((GROUP,)),
        pltpu.SemaphoreType.DMA((GROUP,)),
        pltpu.SemaphoreType.DMA((NY,)),
        pltpu.SemaphoreType.DMA((NY,)),
        pltpu.SemaphoreType.DMA((GROUP,)),
        pltpu.SemaphoreType.DMA((GROUP,)),
    ]

    def __init__(self, refs, reverse):
        self.out, self.inc, self.tot, self.tots, self.ans, self.got = refs[:6]
        self.s1, self.r1, self.s2, self.r2, self.s3, self.r3 = refs[6:]
        self.reverse = reverse
        self.s, self.x, self.y, self.m = place()

    def first(self, i):
        to = (self.m + i) % GROUP
        return copy_to(
            self.out.at[to], self.inc.at[self.m], self.s1.at[i], self.r1.at[i], self.y * GROUP + to, self.x
        )

    def second(self, i):
        to = (self.y + i) % NY
        return copy_to(self.tot, self.tots.at[self.y], self.s2.at[i], self.r2.at[i], to * GROUP + self.m, self.x)

    def third(self, i):
        to = (self.m + i) % GROUP
        return copy_to(
            self.ans.at[to], self.got.at[self.m], self.s3.at[i], self.r3.at[i], self.y * GROUP + to, self.x
        )

    @staticmethod
    def each(count, act):
        def body(i, carry):
            act(i)
            return carry

        lax.fori_loop(1, count, body, 0)

    def fill(self, state, decay):
        for b in range(8):
            lanes = slice(128 * b, 128 * b + 128)
            for k in range(4):
                self.out[:, k, b, :] = state[GROUP * k : GROUP * k + GROUP, lanes]
            self.out[:, 4, b, :] = jnp.broadcast_to(decay[0:1, lanes], (GROUP, 128))

    def start(self):
        self.each(GROUP, lambda i: self.first(i).start())
        self.inc[pl.ds(self.m, 1)] = self.out[pl.ds(self.m, 1)]

    def fold(self):
        self.each(GROUP, lambda i: self.first(i).wait())

        def body(i, carry):
            total, decay = carry
            j = GROUP - 1 - i if self.reverse else i
            block = self.inc[pl.ds(j, 1)][0]
            self.inc[pl.ds(j, 1), 0:4] = total[None]
            self.inc[pl.ds(j, 1), 4:5] = decay[None, None]
            factor = block[4]
            return factor[None] * total + block[0:4], factor * decay

        total, decay = lax.fori_loop(0, GROUP, body, (jnp.zeros((4, 8, 128), F32), jnp.ones((8, 128), F32)))
        self.tot[0:4] = total
        self.tot[4:5] = decay[None]
        self.each(NY, lambda i: self.second(i).start())
        self.tots[pl.ds(self.y, 1), 0:4] = total[None]
        self.tots[pl.ds(self.y, 1), 4:5] = decay[None, None]

    def answer(self):
        self.each(NY, lambda i: self.second(i).wait())
        before = jnp.zeros((4, 8, 128), F32)
        for k in range(NY):
            j = NY - 1 - k if self.reverse else k
            reached = (self.y < j) if self.reverse else (self.y > j)
            block = self.tots[j]
            flag = jnp.full((4, 8, 128), reached.astype(jnp.int32)) > 0
            before = jnp.where(flag, block[4][None] * before + block[0:4], before)

        def body(j, carry):
            block = self.inc[pl.ds(j, 1)][0]
            self.ans[pl.ds(j, 1)] = (block[0:4] + block[4][None] * before)[None]
            return carry

        lax.fori_loop(0, GROUP, body, 0)
        self.each(GROUP, lambda i: self.third(i).start())
        self.got[pl.ds(self.m, 1)] = self.ans[pl.ds(self.m, 1)]

    def finish(self, state_ref):
        self.each(GROUP, lambda i: self.third(i).wait())
        for b in range(8):
            for k in range(4):
                state_ref[GROUP * k : GROUP * k + GROUP, 128 * b : 128 * b + 128] = self.got[:, k, b, :]


NSTATE = len(StateExchange.SCRATCH)


def forward_kernel(orders, og_ref, x_ref, pairs_ref, steps_ref, decay_ref, grads_ref, state_ref, out, inc, ssem, rsem, *refs):
    s, x, _, _ = place()
    barrier = pltpu.get_barrier_semaphore()

    def greet(i, carry):
        pl.semaphore_signal(barrier, inc=1, device_id={"seq": (s + i) % SEQ, "dp": x}, device_id_type=MESH)
        return carry

    lax.fori_loop(1, SEQ, greet, 0)

    states = StateExchange(refs, False)
    _, down, half = scales(steps_ref[...], decay_ref[...])
    fresh = mm_exact_left(pairs_ref[:, 0:STATE], down * x_ref[...].astype(F32), 0, 0)
    states.fill(half[0:1] * fresh, half * half)

    flip_rows = (orders[0] + orders[1]) % 2
    flip_columns = (orders[0] // 2 + orders[1] // 2 + s) % 2
    row = iota((4 * T, T), 0)
    device, quarter, line = row // 16, (row // 4) % 4, row % 4
    token = line * SEQ + jnp.where((line + flip_rows) % 2 == 0, device, SEQ - 1 - device)
    column = iota((4 * T, T), 1)
    packed = jnp.zeros((4 * T, T), F32)
    for j in range(4):
        pick = jnp.where((token == column) & (quarter == j), 1.0, 0.0).astype(BF16)
        packed = packed + mm(pick, og_ref[:, 256 * j : 256 * j + 256])
    out[...] = packed.astype(BF16).reshape(SEQ, 16, 256)

    pl.semaphore_wait(barrier, SEQ - 1)
    states.start()

    def swap(i):
        to = (s + i) % SEQ
        return copy_to(out.at[to], inc.at[s], ssem.at[i], rsem.at[i], to, x)

    StateExchange.each(SEQ, lambda i: swap(i).start())
    inc[pl.ds(s, 1)] = out[pl.ds(s, 1)]
    states.fold()
    states.answer()
    states.finish(state_ref)
    StateExchange.each(SEQ, lambda i: swap(i).wait())

    arrived = inc[...].reshape(4 * T, 256)
    place_ = iota((T, 4 * T), 0)
    source = jnp.where(flip_columns == 0, place_, T - 1 - place_)
    source = (source // 4) * 16 + source % 4
    column = iota((T, 4 * T), 1)
    for j in range(4):
        pick = jnp.where(source + 4 * j == column, 1.0, 0.0).astype(BF16)
        grads_ref[:, 256 * j : 256 * j + 256] = mm(pick, arrived).astype(BF16)


def middle_kernel(
    x_ref, z_ref, pairs_ref, steps_ref, decay_ref, skip_ref, gain_ref, weight_ref, grads_ref, state_ref,
    gate_grad_ref, normed_ref, d_mixed_ref, returns_ref, sums_ref,
):
    up, down, half = scales(steps_ref[...], decay_ref[...])
    x = x_ref[...].astype(F32)
    b, c = pairs_ref[:, 0:STATE], pairs_ref[:, STATE : 2 * STATE]
    lower = iota((T, T), 0) >= iota((T, T), 1)
    mixing = jnp.where(lower, mm(c, b, 1, 1), 0.0)
    inner = mm_split(mixing, down * x) + mm_exact_left(c, half[0:1] * state_ref[...])
    skip = expand(jnp.broadcast_to(skip_ref[...], (8, HEADS)))[0:1]
    mixed = up * inner + skip * x
    gate = z_ref[...].astype(F32)
    sigma = jax.nn.sigmoid(gate)
    active = gate * sigma
    gated = mixed * active
    inverse = lax.rsqrt(jnp.mean(gated * gated, axis=1, keepdims=True) + EPSILON)
    unit = gated * inverse
    gain = gain_ref[...]
    normed_ref[...] = (unit * gain).astype(BF16)
    d_normed = mm(grads_ref[...], weight_ref[...], 1, 1)
    scaled = d_normed * gain
    d_gated = inverse * (scaled - unit * jnp.mean(scaled * unit, axis=1, keepdims=True))
    gate_grad_ref[...] = (d_gated * mixed * sigma * (1.0 + gate * (1.0 - sigma))).astype(BF16)
    d_mixed = d_gated * active
    d_mixed_ref[...] = d_mixed
    sums_ref[0:1] = jnp.sum(d_normed * unit, axis=0, keepdims=True)
    sums_ref[1:2] = jnp.sum(d_mixed * x, axis=0, keepdims=True)
    returns_ref[...] = half[0:1] * mm_exact_left(c, up * d_mixed, 0, 0)


def backward_kernel(
    normed_ref, grads_ref, returns_ref, steps_ref, decay_ref, sums_ref,
    full, leaving_ref, total_ref,
    peer_normed, peer_grads, mine, rough, a1, b1, ra1, rb1, ra2, rb2, c1, r3, g3,
    t0, t1, t2, t3, tr0, tr1, tr2, tr3,
    s0, q0, sa, qa, sb, qb, sa2, qa2, sb2, qb2, s3, q3, s4, q4, sa5, qa5, sb5, qb5, sa6, qa6, sb6, qb6, s7, q7,
    ts0, tq0, ts1, tq1, ts2, tq2, ts3, tq3,
    *refs,
):
    s, x, y, m = place()
    z, core = m // 2, m % 2
    other = s + 1 - 2 * core
    barrier = pltpu.get_barrier_semaphore()

    def hello(seq, dp):
        pl.semaphore_signal(barrier, inc=1, device_id={"seq": seq, "dp": dp}, device_id_type=MESH)

    StateExchange.each(GROUP, lambda i: hello(y * GROUP + (m + i) % GROUP, x))
    StateExchange.each(NY, lambda i: hello(((y + i) % NY) * GROUP + m, x))
    StateExchange.each(NX, lambda i: hello(s, (x + i) % NX))

    states = StateExchange(refs, True)
    _, _, half = scales(steps_ref[...], decay_ref[...])
    states.fill(returns_ref[...], half * half)
    t0[...] = jnp.zeros_like(t0)
    t0[0:2] = sums_ref[...]
    pl.semaphore_wait(barrier, GROUP - 1 + NY - 1 + NX - 1)

    def along_x(i):
        return s, (x + i) % NX

    def along_y(i):
        return ((y + i) % NY) * GROUP + m, x

    def along_z(i):
        return y * GROUP + ((z + i) % NZ) * 2 + core, x

    def sum_round(count, out, inc, ss, rr, peer):
        return [copy_to(out, inc.at[i - 1], ss.at[i], rr.at[i], *peer(i)) for i in range(1, count)]

    def begin(copies):
        for one in copies:
            one.start()

    def end(copies):
        for one in copies:
            one.wait()

    pair = [
        copy_to(grads_ref, peer_grads, s0.at[0], q0.at[0], other, x),
        copy_to(
            normed_ref.at[:, pl.ds(pl.multiple_of((1 - core) * 512, 512), 512)],
            peer_normed, s0.at[1], q0.at[1], other, x,
        ),
        copy_to(t0, tr0, ts0.at[0], tq0.at[0], other, x),
    ]
    begin(pair)
    states.start()
    own = normed_ref[:, pl.ds(pl.multiple_of(core * 512, 512), 512)]
    mine[...] = mm(own, grads_ref[...], 0, 0)
    end(pair)
    mine[...] += mm(peer_normed[...], peer_grads[...], 0, 0)
    rough[...] = mine[...].astype(BF16)
    t1[...] = t0[...] + tr0[...]

    left, right = pl.ds(0, 512), pl.ds(512, 512)

    def rows(i, size, base=0):
        return pl.ds(pl.multiple_of(base + i * size, size), size)

    first = []
    for i in range(1, NX):
        first.append(copy_to(rough.at[rows((x + i) % NX, 128), left], ra1.at[i - 1], sa.at[i], qa.at[i], *along_x(i)))
        first.append(copy_to(rough.at[rows((y + i) % NY, 128), right], rb1.at[i - 1], sb.at[i], qb.at[i], *along_y(i)))
    first += sum_round(NX, t1, tr1, ts1, tq1, along_x)
    begin(first)
    states.fold()
    end(first)
    a1[...] = mine[rows(x, 128), 0:512] + (ra1[0].astype(F32) + ra1[1].astype(F32) + ra1[2].astype(F32))
    b1[...] = mine[rows(y, 128), 512:1024] + (rb1[0].astype(F32) + rb1[1].astype(F32) + rb1[2].astype(F32))
    t2[...] = t1[...] + tr1[0] + tr1[1] + tr1[2]
    second = []
    for i in range(1, NY):
        second.append(copy_to(a1.at[rows((y + i) % NY, 32)], ra2.at[i - 1], sa2.at[i], qa2.at[i], *along_y(i)))
        second.append(copy_to(b1.at[rows((x + i) % NX, 32)], rb2.at[i - 1], sb2.at[i], qb2.at[i], *along_x(i)))
    second += sum_round(NY, t2, tr2, ts2, tq2, along_y)
    begin(second)
    states.answer()
    end(second)
    a2 = a1[rows(y, 32), :] + ra2[0] + ra2[1] + ra2[2]
    b2 = b1[rows(x, 32), :] + rb2[0] + rb2[1] + rb2[2]
    t3[...] = t2[...] + tr2[0] + tr2[1] + tr2[2]
    for k in range(4):
        part = (slice(16 * (k // 2), 16 * (k // 2) + 16), slice(256 * (k % 2), 256 * (k % 2) + 256))
        c1[k] = a2[part]
        c1[k + 4] = b2[part]
    third = [
        copy_to(c1.at[(z + i) % NZ], r3.at[i - 1], s3.at[i], q3.at[i], *along_z(i)) for i in range(1, NZ)
    ] + sum_round(NZ, t3, tr3, ts3, tq3, along_z)
    begin(third)
    states.finish(leaving_ref)
    end(third)
    block = c1[pl.ds(z, 1)][0]
    total = t3[...]
    for i in range(NZ - 1):
        block = block + r3[i]
        total = total + tr3[i]
    total_ref[...] = total[0:2]
    g3[pl.ds(z, 1)] = block.astype(BF16)[None]
    fourth = [
        copy_to(g3.at[z], g3.at[z], s4.at[i], q4.at[i], *along_z(i)) for i in range(1, NZ)
    ]
    begin(fourth)
    end(fourth)
    base = core * 512
    for k in range(4):
        lanes = slice(256 * (k % 2), 256 * (k % 2) + 256)
        full[rows(k // 2, 16, base + 128 * x + 32 * y), lanes] = g3[k]
        lanes = slice(512 + 256 * (k % 2), 512 + 256 * (k % 2) + 256)
        full[rows(k // 2, 16, base + 128 * y + 32 * x), lanes] = g3[k + 4]
    fifth = []
    at_a = full.at[rows(y, 32, base + 128 * x), left]
    at_b = full.at[rows(x, 32, base + 128 * y), right]
    for i in range(1, NX):
        fifth.append(copy_to(at_a, at_a, sa5.at[i], qa5.at[i], *along_y(i)))
        fifth.append(copy_to(at_b, at_b, sb5.at[i], qb5.at[i], *along_x(i)))
    begin(fifth)
    end(fifth)
    at_a = full.at[rows(x, 128, base), left]
    at_b = full.at[rows(y, 128, base), right]
    sixth = []
    for i in range(1, NX):
        sixth.append(copy_to(at_a, at_a, sa6.at[i], qa6.at[i], *along_x(i)))
        sixth.append(copy_to(at_b, at_b, sb6.at[i], qb6.at[i], *along_y(i)))
    begin(sixth)
    last = []

    def hand_over(at, k):
        one = copy_to(at, at, s7.at[k], q7.at[k], other, x)
        one.start()
        last.append(one)

    hand_over(at_a, 0)
    hand_over(at_b, 1)
    for i in range(1, NX):
        sixth[2 * i - 2].wait()
        hand_over(full.at[rows((x + NX - i) % NX, 128, base), left], 2 * i)
        sixth[2 * i - 1].wait()
        hand_over(full.at[rows((y + NY - i) % NY, 128, base), right], 2 * i + 1)
    end(last)


def final_kernel(
    x_ref, pairs_ref, steps_ref, decay_ref, skip_ref, d_mixed_ref, state_ref, leaving_ref, input_grad_ref, pair_grad_ref
):
    up, down, half = scales(steps_ref[...], decay_ref[...])
    b, c = pairs_ref[:, 0:STATE], pairs_ref[:, STATE : 2 * STATE]
    lower = iota((T, T), 0) >= iota((T, T), 1)
    mixing = jnp.where(lower, mm(c, b, 1, 1), 0.0)
    d_mixed = d_mixed_ref[...]
    pulled = up * d_mixed
    pushed = down * x_ref[...].astype(F32)
    entering = half[0:1] * state_ref[...]
    leaving = half[0:1] * leaving_ref[...]
    skip = expand(jnp.broadcast_to(skip_ref[...], (8, HEADS)))[0:1]
    d_x = down * (mm_split(mixing, pulled, 0, 0) + mm_exact_left(b, leaving)) + skip * d_mixed
    input_grad_ref[...] = d_x.astype(BF16)
    paired = jnp.where(lower, mm_split(pulled, pushed, 1, 1), 0.0)
    d_b = mm_exact_right(paired, c, 0, 0) + mm_split(pushed, leaving, 1, 1)
    d_c = mm_exact_right(paired, b) + mm_split(pulled, entering, 1, 1)
    pair_grad_ref[:, 0:STATE] = d_b.astype(BF16)
    pair_grad_ref[:, STATE : 2 * STATE] = d_c.astype(BF16)


VM = pl.BlockSpec(memory_space=pltpu.VMEM)
SM = pl.BlockSpec(memory_space=pltpu.SMEM)


def call(kernel, outs, args, specs=None, scratch=(), collective=None):
    extra = {} if collective is None else dict(collective_id=collective, has_side_effects=True)
    return pl.pallas_call(
        kernel,
        out_shape=[jax.ShapeDtypeStruct(shape, kind) for shape, kind in outs],
        in_specs=specs or [VM] * len(args),
        out_specs=[VM] * len(outs),
        scratch_shapes=list(scratch),
        compiler_params=pltpu.CompilerParams(vmem_limit_bytes=VMEM_LIMIT, **extra),
    )(*args)


def sems(*counts):
    return [pltpu.SemaphoreType.DMA((n,)) for n in counts for _ in range(2)]


def local(inputs, gates, pairs, steps, log_decay, skip, gain, out_weight, out_grad, order_ids):
    x, z, bc, dt, og = inputs[0], gates[0], pairs[0], steps[0], out_grad[0]
    decay, skip_row, gain_row = log_decay[None], skip[None], gain[None]
    grads, entering = call(
        forward_kernel,
        [((T, W), BF16), ((STATE, W), F32)],
        (order_ids, og, x, bc, dt, decay),
        [SM] + [VM] * 5,
        [pltpu.VMEM((SEQ, 16, 256), BF16)] * 2 + sems(SEQ) + StateExchange.SCRATCH,
        0,
    )
    gate_grad, normed, d_mixed, returns, sums = call(
        middle_kernel,
        [((T, W), BF16), ((T, W), BF16), ((T, W), F32), ((STATE, W), F32), ((2, W), F32)],
        (x, z, bc, dt, decay, skip_row, gain_row, out_weight, grads, entering),
    )
    tiny = pltpu.VMEM((8, W), F32)
    full, leaving, total = call(
        backward_kernel,
        [((W, W), BF16), ((STATE, W), F32), ((2, W), F32)],
        (normed, grads, returns, dt, decay, sums),
        None,
        [
            pltpu.VMEM((T, 512), BF16),
            pltpu.VMEM((T, W), BF16),
            pltpu.VMEM((512, W), F32),
            pltpu.VMEM((512, W), BF16),
            pltpu.VMEM((128, 512), F32),
            pltpu.VMEM((128, 512), F32),
            pltpu.VMEM((3, 128, 512), BF16),
            pltpu.VMEM((3, 128, 512), BF16),
            pltpu.VMEM((3, 32, 512), F32),
            pltpu.VMEM((3, 32, 512), F32),
            pltpu.VMEM((8, 16, 256), F32),
            pltpu.VMEM((7, 16, 256), F32),
            pltpu.VMEM((8, 16, 256), BF16),
            tiny, tiny, tiny, tiny, tiny,
            pltpu.VMEM((3, 8, W), F32),
            pltpu.VMEM((3, 8, W), F32),
            pltpu.VMEM((7, 8, W), F32),
        ]
        + sems(2, 4, 4, 4, 4, 8, 8, 4, 4, 4, 4, 8, 1, 4, 4, 8)
        + StateExchange.SCRATCH,
        1,
    )
    input_grad, pair_grad = call(
        final_kernel,
        [((T, W), BF16), ((T, 2 * STATE), BF16)],
        (x, bc, dt, decay, skip_row, d_mixed, entering, leaving),
    )
    skip_grad = jnp.sum(total[1].reshape(HEADS, W // HEADS), axis=1)
    return input_grad[None], gate_grad[None], pair_grad[None], full.astype(F32), total[0], skip_grad


def solution(mesh):
    token = P("dp", "seq", None)
    return jax.shard_map(
        local,
        mesh=mesh,
        in_specs=(token, token, token, P("dp", None, "seq"), P(), P(), P(), P(), token, P()),
        out_specs=(token, token, token, P(), P(), P()),
        check_vma=False,
    )
```

time: 899 us -> 121 us (0.13)
  blocking collectives: 331 us -> 0 us
  other arithmetic: 230 us -> 3.11 us
  waiting for transfers between devices: 173 us -> 0 us
  Pallas kernels: 0 us -> 116 us
  local copies, waits for them, and re-layouts: 90.7 us -> 0.68 us
  matrix products: 30.1 us -> 0 us
  between operations: 20.4 us -> 0.67 us
  starting transfers between devices: 13.7 us -> 0 us
    unnamed x2 -> x0, blocking collectives: 258 us -> none
    select_n x131 -> x0, other arithmetic: 212 us -> none  [the longest x128 211 us: step(): return jax.tree.map(lambda a, b: jnp.where(reached, a, b), new, before)]
    psum x1 -> x0, waiting for transfers between devices: 173 us -> none  [local(): lax.psum((weight_term, gain_part, skip_part), ('seq', 'dp'))]
    pallas_call x0 -> x4, Pallas kernels: none -> 116 us  [call(): pl.pallas_call(kernel, out_shape=[jax.ShapeDtypeStruct(shape, kind) for s...]
    psum x1 -> x0, blocking collectives: 73.7 us -> none  [local(): lax.psum((weight_term, gain_part, skip_part), ('seq', 'dp'))]
    mul x130 -> x0, local copies, waits for them, and re-layouts: 45.3 us -> none  [the longest x128 44.9 us: combine_states(): later[0][:, None, None] * earlier[1] + later[1]]
    dot_general x14 -> x0, matrix products: 30.1 us -> none  [the longest x1 5.14 us: local(): jnp.einsum('chi,chpn,cin->cihp', growth, starts, input_c_matrix, precisio...]
    all_to_all x1 -> x0, starting transfers between devices: 13.3 us -> none  [local(): lax.all_to_all(outgoing, 'seq', split_axis=1, concat_axis=2, tiled=True)]
  transfers between devices with their start and end apart: 4 -> 0, of which waited for: 1 -> 0; matrix products, arithmetic and copies ran while one was open for 14% -> 0% of each run, Pallas kernels for 0% -> 0%
where the time goes in v1:
time: 121 us
  Pallas kernels  116 us (96%)
  other arithmetic  3.11 us (3%)
    pallas_call x4, Pallas kernels, call(): pl.pallas_call(kernel, out_shape=[jax.ShapeDtypeStruct(shape, kind) for s...  116 us
    convert_element_type x1, other arithmetic, local(): full.astype(F32)  2.48 us

profile of v1, /device:TPU:1, one launch (start us, length us, event | category | flops | bytes accessed | tf_op | source)
XLA Modules:
  0.0 120.6 jit_solution(9011260450060607492)
XLA Ops:
  0.6 43.0 %shard_map.145 = (bf16[256,1024]{1,0:T(8,128)(2,1)}, f32[64,1024]{1,0:T(8,128)}) custom-call(s32[2]{0:T(128)} %orders.1, bf16[256,1024]{1,0:T(8,128)(2,1)} %bitcast.18, bf16[256,1024]{1,0:T(8,128)(2,1)} %bitcast.12, bf16[256,128]{1,0:T(8,128)(2,1)} %bitcast.15, f32[16,256]{1,0:T(8,128)} %bitcast.20, f32[1,16]{1,0:T(1,128)} %bitcast.24), custom_call_target="tpu_custom_call" | custom-call | tf_op jit(solution)/shard_map/pallas_call | solution.py:455
  43.6 7.5 %shard_map.146 = (bf16[256,1024]{1,0:T(8,128)(2,1)}, bf16[256,1024]{1,0:T(8,128)(2,1)}, f32[256,1024]{1,0:T(8,128)}, f32[64,1024]{1,0:T(8,128)}, f32[2,1024]{1,0:T(2,128)}) custom-call(bf16[256,1024]{1,0:T(8,128)(2,1)} %bitcast.13, bf16[256,1024]{1,0:T(8,128)(2,1)} %bitcast.19, bf16[256,128]{1,0:T(8,128)(2,1)} %bitcast.16, f32[16,256]{1,0:T(8,128)} %bitcast.21, ...), custom_call_target="tpu_custom_call" | custom-call | tf_op jit(solution)/shard_map/pallas_call | solution.py:455
  51.1 59.1 %shard_map.147 = (bf16[1024,1024]{1,0:T(8,128)(2,1)}, f32[64,1024]{1,0:T(8,128)}, f32[2,1024]{1,0:T(2,128)}) custom-call(bf16[256,1024]{1,0:T(8,128)(2,1)} %get-tuple-element.21.normed_ref, bf16[256,1024]{1,0:T(8,128)(2,1)} %get-tuple-element.18.grads_ref, f32[64,1024]{1,0:T(8,128)} %get-tuple-element.22.returns_ref, f32[16,256]{1,0:T(8,128)} %bitcast.22, ...), custom_call_target="tpu_custom_call" | custom-call | tf_op jit(solution)/shard_map/pallas_call | solution.py:455
  110.3 0.0 copy-start.1
  110.3 0.0 copy-start
  110.3 6.5 %shard_map.148 = (bf16[256,1024]{1,0:T(8,128)(2,1)}, bf16[256,128]{1,0:T(8,128)(2,1)}) custom-call(bf16[256,1024]{1,0:T(8,128)(2,1)} %bitcast.14, bf16[256,128]{1,0:T(8,128)(2,1)} %bitcast.17, f32[16,256]{1,0:T(8,128)} %bitcast.23, f32[1,16]{1,0:T(1,128)} %bitcast.27, f32[1,16]{1,0:T(1,128)} %bitcast.31, f32[256,1024]{1,0:T(8,128)} %get-tuple-element.20.d_mixed_ref, ...), custom_call_target="tpu_custom_call" | custom-call | tf_op jit(solution)/shard_map/pallas_call | solution.py:455
  116.8 0.0 copy-done.1
  116.8 0.6 slice_reduce_fusion
  117.4 0.1 reshape_squeeze.3
  117.5 0.6 reduce_sum.9
  118.1 0.0 copy-done
  118.1 2.5 %convert_element_type.3 = f32[1024,1024]{1,0:T(8,128)} convert(bf16[1024,1024]{1,0:T(8,128)(2,1)S(1)} %copy-done) | non-fusion elementwise | flops 1048576 | bytes 6291456 | tf_op jit(solution)/shard_map/convert_element_type | solution.py:520
Async XLA Ops:
  110.3 6.5 %copy-start.1 = (f32[2,1024]{1,0:T(2,128)S(1)}, f32[2,1024]{1,0:T(2,128)}, u32[]{:S(2)}) copy-start(f32[2,1024]{1,0:T(2,128)} %get-tuple-element.29) | copy-start | bytes 24580
  110.3 7.8 %copy-start = (bf16[1024,1024]{1,0:T(8,128)(2,1)S(1)}, bf16[1024,1024]{1,0:T(8,128)(2,1)}, u32[]{:S(2)}) copy-start(bf16[1024,1024]{1,0:T(8,128)(2,1)} %get-tuple-element.28) | copy-start | bytes 6291460

commit v2 on v0

v2 whole, which is shorter than its diff:
```python
import types

import jax
import jax.numpy as jnp
from jax import lax
from jax.experimental import pallas as pl
from jax.experimental.pallas import tpu as pltpu
from jax.sharding import PartitionSpec as P

F32 = jnp.float32
BF16 = jnp.bfloat16
MESH = pl.DeviceIdType.MESH
EPSILON = 1e-05
T = 256
W = 1024
HEADS = 16
STATE = 64
SEQ, NX, NY, NZ, GROUP = 64, 4, 4, 8, 16
VMEM_LIMIT = 56 * 1024 * 1024


def iota(shape, dim):
    return lax.broadcasted_iota(jnp.int32, shape, dim)


def mm(a, b, ca=1, cb=0):
    return lax.dot_general(a, b, (((ca,), (cb,)), ((), ())), preferred_element_type=F32)


def split(a):
    high = a.astype(BF16)
    return high, (a - high.astype(F32)).astype(BF16)


def mm_exact_left(a, b, ca=1, cb=0):
    high, low = split(b)
    return mm(a, high, ca, cb) + mm(a, low, ca, cb)


def mm_exact_right(a, b, ca=1, cb=0):
    high, low = split(a)
    return mm(high, b, ca, cb) + mm(low, b, ca, cb)


def mm_split(a, b, ca=1, cb=0):
    ah, al = split(a)
    bh, bl = split(b)
    return mm(ah, bh, ca, cb) + (mm(ah, bl, ca, cb) + mm(al, bh, ca, cb))


def terms(a):
    high = a.astype(BF16)
    rest = a - high.astype(F32)
    mid = rest.astype(BF16)
    return high, mid, (rest - mid.astype(F32)).astype(BF16)


def expand(small):
    spread = (iota((HEADS, W), 1) // (W // HEADS) == iota((HEADS, W), 0)).astype(F32).astype(BF16)
    high, mid, low = terms(small)
    return mm(high, spread) + (mm(mid, spread) + mm(low, spread))


def scales(steps, log_decay):
    token_steps = steps.T
    lower = (iota((T, T), 0) >= iota((T, T), 1)).astype(F32).astype(BF16)
    high, mid, low = terms(token_steps * (-jnp.exp(log_decay)))
    logs = mm(lower, high) + (mm(lower, mid) + mm(lower, low))
    mid = 0.5 * logs[T - 1 : T, :]
    down = expand(jnp.exp(mid - logs) * token_steps)
    half = expand(jnp.broadcast_to(jnp.exp(mid), (8, HEADS)))
    return jnp.exp(logs - mid), down, half


def place():
    s = lax.axis_index("seq")
    return s, lax.axis_index("dp"), s // GROUP, s % GROUP


def copy_to(src, dst, send, recv, seq, dp):
    return pltpu.make_async_remote_copy(
        src_ref=src, dst_ref=dst, send_sem=send, recv_sem=recv, device_id={"seq": seq, "dp": dp}, device_id_type=MESH
    )


def each(count, act, start=1):
    def body(i, carry):
        act(i)
        return carry

    lax.fori_loop(start, count, body, 0)


def far_first(count):
    return sorted(range(1, count), key=lambda i: -min(i, count - i))


def begin(copies):
    for one in copies:
        one.start()


def end(copies):
    for one in copies:
        one.wait()


def rows(i, size, base=0):
    return pl.ds(pl.multiple_of(base + i * size, size), size)


def dma(*count):
    return pltpu.SemaphoreType.DMA(count)


class StateExchange:
    def __init__(self, ref, wire, reverse):
        self.ref, self.reverse, self.wire = ref, reverse, wire
        self.s, self.x, self.y, m = place()
        self.m, self.z, self.core = m, m // 2, m % 2
        self.other = self.s + 1 - 2 * self.core
        self.early = self.core == (1 if reverse else 0)

    @staticmethod
    def scratch(wire, back):
        tiles = 5 if wire == F32 else 6
        return dict(
            stage=pltpu.VMEM((2, NZ, 4, 8, 128), F32),
            decay=pltpu.VMEM((8, 128), F32),
            peer=pltpu.VMEM((NZ, 4, 8, 128), F32),
            peer_decay=pltpu.VMEM((8, 128), F32),
            out=pltpu.VMEM((NZ, 8 * tiles, 128), wire),
            inc=pltpu.VMEM((NZ, 8 * tiles, 128), wire),
            fold=pltpu.VMEM((NZ, tiles, 8, 128), F32),
            tot=pltpu.VMEM((5, 8, 128), F32),
            tots=pltpu.VMEM((NY, 5, 8, 128), F32),
            ans=pltpu.VMEM((NZ, 32, 128), back),
            got=pltpu.VMEM((NZ, 32, 128), back),
            give=pltpu.VMEM((NZ, 4, 8, 128), F32),
            take=pltpu.VMEM((NZ, 4, 8, 128), F32),
            s0=dma(3),
            r0=dma(3),
            s1=dma(NZ),
            r1=dma(NZ),
            s2=dma(NY),
            r2=dma(NY),
            s3=dma(NZ),
            r3=dma(NZ),
        )

    def pair(self, k):
        r = self.ref
        src, dst = ((r.stage.at[1 - self.core], r.peer), (r.decay, r.peer_decay), (r.give, r.take))[k]
        return copy_to(src, dst, r.s0.at[k], r.r0.at[k], self.other, self.x)

    def along_z(self, src, dst, send, recv, i):
        to = (self.z + i) % NZ
        return copy_to(
            src.at[to], dst.at[self.z], send.at[i], recv.at[i], self.y * GROUP + to * 2 + self.core, self.x
        )

    def first(self, i):
        return self.along_z(self.ref.out, self.ref.inc, self.ref.s1, self.ref.r1, i)

    def second(self, i):
        r, to = self.ref, (self.y + i) % NY
        return copy_to(r.tot, r.tots.at[self.y], r.s2.at[i], r.r2.at[i], to * GROUP + self.m, self.x)

    def third(self, i):
        return self.along_z(self.ref.ans, self.ref.got, self.ref.s3, self.ref.r3, i)

    def start(self, state, decay):
        r = self.ref
        for b in range(8):
            lanes = slice(128 * b, 128 * b + 128)
            r.decay[b : b + 1] = decay[0:1, lanes]
            for k in range(4):
                for core in range(2):
                    at = 16 * k + 8 * core
                    r.stage[core, :, k, b, :] = state[at : at + 8, lanes]

    def share(self):
        begin([self.pair(1), self.pair(0)])

    def send(self):
        r = self.ref
        end([self.pair(1), self.pair(0)])
        own, peer = r.stage[pl.ds(self.core, 1)][0], r.peer[...]
        mine, theirs = r.decay[...], r.peer_decay[...]
        early = jnp.full((8, 128), self.early.astype(jnp.int32)) > 0
        own_factor, peer_factor = jnp.where(early, theirs, 1.0), jnp.where(early, 1.0, mine)
        r.fold[:, 0:4] = own_factor * own + peer_factor * peer
        both = mine * theirs
        if self.wire == F32:
            r.fold[:, 4] = jnp.broadcast_to(both, (NZ, 8, 128))
        else:
            high = both.astype(BF16).astype(F32)
            r.fold[:, 4] = jnp.broadcast_to(high, (NZ, 8, 128))
            r.fold[:, 5] = jnp.broadcast_to(both - high, (NZ, 8, 128))
        r.out[...] = r.fold[...].reshape(r.out.shape).astype(self.wire)
        begin([self.first(i) for i in far_first(NZ)])
        r.inc[pl.ds(self.z, 1)] = r.out[pl.ds(self.z, 1)]

    def fold(self):
        r = self.ref
        end([self.first(i) for i in far_first(NZ)])
        r.fold[...] = r.inc[...].astype(F32).reshape(r.fold.shape)
        total, decay = jnp.zeros((4, 8, 128), F32), jnp.ones((8, 128), F32)
        for j in range(NZ)[:: -1 if self.reverse else 1]:
            block = r.fold[j]
            r.fold[j, 0:4] = total
            r.fold[j, 4] = decay
            factor = block[4] if self.wire == F32 else block[4] + block[5]
            total, decay = factor[None] * total + block[0:4], factor * decay
        r.tot[0:4] = total
        r.tot[4] = decay
        begin([self.second(i) for i in far_first(NY)])
        r.tots[pl.ds(self.y, 1)] = r.tot[...][None]

    def answer(self):
        r = self.ref
        end([self.second(i) for i in far_first(NY)])
        before = jnp.zeros((4, 8, 128), F32)
        for j in range(NY)[:: -1 if self.reverse else 1]:
            reached = (self.y < j) if self.reverse else (self.y > j)
            flag = jnp.full((4, 8, 128), reached.astype(jnp.int32)) > 0
            before = jnp.where(flag, r.tots[j, 4][None] * before + r.tots[j, 0:4], before)
        answers = r.fold[:, 0:4] + r.fold[:, 4:5] * before[None]
        r.ans[...] = answers.reshape(r.ans.shape).astype(r.ans.dtype)
        begin([self.third(i) for i in far_first(NZ)])
        r.got[pl.ds(self.z, 1)] = r.ans[pl.ds(self.z, 1)]

    def halve(self):
        r = self.ref
        end([self.third(i) for i in far_first(NZ)])
        entering = r.got[...].astype(F32).reshape(NZ, 4, 8, 128)
        own, peer = r.stage[pl.ds(self.core, 1)][0], r.peer[...]
        early = jnp.full((NZ, 4, 8, 128), self.early.astype(jnp.int32)) > 0
        r.give[...] = jnp.where(early, r.decay[...] * entering + own, entering)
        begin([self.pair(2)])
        r.stage[pl.ds(self.core, 1)] = jnp.where(early, entering, r.peer_decay[...] * entering + peer)[None]

    def finish(self, state_ref, scale):
        r = self.ref
        end([self.pair(2)])
        r.stage[pl.ds(1 - self.core, 1)] = r.take[...][None]
        for b in range(8):
            lanes = slice(128 * b, 128 * b + 128)
            for k in range(4):
                for core in range(2):
                    at = 16 * k + 8 * core
                    state_ref[at : at + 8, lanes] = r.stage[core, :, k, b, :] * scale[:, lanes]


class Ring:
    def __init__(self, ref, me, device):
        self.ref, self.me, self.right, self.left = ref, me, device(1), device(3)

    @staticmethod
    def scratch():
        half, whole = pltpu.VMEM((64, 512), BF16), pltpu.VMEM((128, 512), BF16)
        return dict(
            in_left=half, in_right=half, to_right=half, to_left=half, from_left=whole, from_right=whole,
            s1=dma(6), r1=dma(6), s6=dma(6), r6=dma(6),
        )

    def one(self, k, src, dst, device, send, recv):
        return copy_to(src, dst, send.at[k], recv.at[k], *device)

    def start_sum(self, rough, lanes):
        r, me = self.ref, self.me
        far, right, left = 128 * ((me + 2) % 4), 128 * ((me + 1) % 4), 128 * ((me + 3) % 4)
        top, low = slice(0, 64), slice(64, 128)
        parts = (
            (rough.at[rows(0, 64, far), lanes], r.in_left, self.right),
            (rough.at[rows(1, 64, far), lanes], r.in_right, self.left),
            (rough.at[rows(1, 64, right), lanes], r.from_left.at[low], self.right),
            (rough.at[rows(0, 64, left), lanes], r.from_right.at[top], self.left),
            (r.to_right, r.from_left.at[top], self.right),
            (r.to_left, r.from_right.at[low], self.left),
        )
        self.sums = [self.one(k, *part, r.s1, r.r1) for k, part in enumerate(parts)]
        begin(self.sums[0:4])

    def pass_sum(self, mine, lanes):
        r, me = self.ref, self.me
        end(self.sums[0:1])
        r.to_right[...] = (mine[rows(0, 64, 128 * ((me + 1) % 4)), lanes] + r.in_left[...].astype(F32)).astype(BF16)
        begin(self.sums[4:5])
        end(self.sums[1:2])
        r.to_left[...] = (mine[rows(1, 64, 128 * ((me + 3) % 4)), lanes] + r.in_right[...].astype(F32)).astype(BF16)
        begin(self.sums[5:6])

    def end_sum(self, mine, lanes):
        r = self.ref
        end(self.sums[2:6])
        return mine[rows(self.me, 128), lanes] + (r.from_left[...].astype(F32) + r.from_right[...].astype(F32))

    def start_gather(self, full, base, lanes):
        r, me = self.ref, self.me

        def half(j, low):
            return full.at[rows(low, 64, base + 128 * ((me + j) % 4)), lanes]

        def send(k, j, low, device):
            return self.one(k, half(j, low), half(j, low), device, r.s6, r.r6)

        self.gathers = [
            send(0, 0, 0, self.right),
            send(1, 0, 1, self.left),
            send(2, 0, 1, self.right),
            send(3, 0, 0, self.left),
            send(4, 3, 0, self.right),
            send(5, 1, 1, self.left),
        ]
        begin(self.gathers[0:4])

    def pass_gather(self):
        end(self.gathers[0:1])
        begin(self.gathers[4:5])
        end(self.gathers[1:2])
        begin(self.gathers[5:6])


def buffers():
    full, half = pltpu.VMEM((T, W), F32), pltpu.VMEM((T, W), BF16)
    out = dict(
        x=half,
        z=half,
        og=half,
        bc=pltpu.VMEM((T, 2 * STATE), BF16),
        dt=pltpu.VMEM((HEADS, T), F32),
        w=pltpu.VMEM((W, W), BF16),
        load=dma(6),
        save=dma(20),
        swap_out=pltpu.VMEM((SEQ, 16, 256), BF16),
        swap_in=pltpu.VMEM((SEQ, 16, 256), BF16),
        swap_s=dma(SEQ),
        swap_r=dma(SEQ),
        grads=half,
        u=pltpu.VMEM((T, HEADS), F32),
        up=full,
        down=full,
        half=pltpu.VMEM((8, W), F32),
        skip=pltpu.VMEM((8, W), F32),
        pushed=full,
        mixing=pltpu.VMEM((T, T), F32),
        inner=full,
        active=full,
        slope=full,
        entering=pltpu.VMEM((STATE, W), F32),
        leaving=pltpu.VMEM((STATE, W), F32),
        inverse=pltpu.VMEM((T, 1), F32),
        unit=full,
        normed=half,
        d_normed=full,
        d_mixed=full,
        pulled=full,
        d_x=full,
        d_b=pltpu.VMEM((T, STATE), F32),
        gate_grad=half,
        input_grad=half,
        pair_grad=pltpu.VMEM((T, 2 * STATE), BF16),
        peer_normed=pltpu.VMEM((T, 512), BF16),
        peer_grads=half,
        pair_s=dma(2),
        pair_r=dma(2),
        mine=pltpu.VMEM((512, W), F32),
        rough=pltpu.VMEM((512, W), BF16),
        a1=pltpu.VMEM((128, 512), F32),
        b1=pltpu.VMEM((128, 512), F32),
        a1_out=pltpu.VMEM((128, 512), BF16),
        b1_out=pltpu.VMEM((128, 512), BF16),
        a2=pltpu.VMEM((3, 32, 512), BF16),
        b2=pltpu.VMEM((3, 32, 512), BF16),
        a2_s=dma(4), a2_r=dma(4), b2_s=dma(4), b2_r=dma(4),
        c1=pltpu.VMEM((8, 16, 256), F32),
        c3=pltpu.VMEM((7, 16, 256), F32),
        c3_s=dma(8), c3_r=dma(8), c4_s=dma(8), c4_r=dma(8),
        c4=pltpu.VMEM((8, 16, 256), BF16),
        a5_s=dma(4), a5_r=dma(4), b5_s=dma(4), b5_r=dma(4),
        full=pltpu.VMEM((W, W), BF16),
        last_s=dma(8), last_r=dma(8),
        sums=pltpu.VMEM((16, 128), F32),
    )
    rounds = [
        dict(
            mine=pltpu.VMEM((16, 128), F32), theirs=pltpu.VMEM((count - 1, 16, 128), F32), s=dma(count), r=dma(count)
        )
        for count in (2, NX, NY, NZ)
    ]
    return [out, StateExchange.scratch(*FORWARD), StateExchange.scratch(*BACKWARD), Ring.scratch(), Ring.scratch(), *rounds]


FORWARD, BACKWARD = (F32, F32), (F32, F32)
BUFFERS = buffers()


def kernel(
    orders, decay_ref, skip_ref, gain_ref, x_in, z_in, bc_in, dt_in, w_in, og_in,
    input_grad_out, gate_grad_out, pair_grad_out, full_out, total_out, *scratch,
):
    scratch = iter(scratch)
    ref, ref_f, ref_b, ring_a, ring_b, *rounds = [
        types.SimpleNamespace(**{key: next(scratch) for key in group}) for group in BUFFERS
    ]
    s, x, y, m = place()
    z, core = m // 2, m % 2
    other = s + 1 - 2 * core

    barrier = pltpu.get_barrier_semaphore()

    def hello(seq, dp):
        pl.semaphore_signal(barrier, inc=1, device_id=dict(seq=seq, dp=dp), device_id_type=MESH)

    operands = ((dt_in, ref.dt), (bc_in, ref.bc), (x_in, ref.x), (og_in, ref.og), (z_in, ref.z), (w_in, ref.w))
    loads = [pltpu.make_async_copy(src, dst, ref.load.at[k]) for k, (src, dst) in enumerate(operands)]
    begin(loads)
    each(SEQ, lambda i: hello((s + i) % SEQ, x))
    each(NX, lambda i: hello(s, (x + i) % NX))

    end(loads[0:1])
    ref.u[...], down, half = scales(ref.dt[...], decay_ref[...])
    ref.down[...], ref.half[...] = down, half
    end(loads[1:3])
    ref.pushed[...] = down * ref.x[...].astype(F32)
    forward = StateExchange(ref_f, FORWARD[0], False)
    b, c = ref.bc[:, 0:STATE], ref.bc[:, STATE : 2 * STATE]
    forward.start(half[0:1] * mm_exact_left(b, ref.pushed[...], 0, 0), half * half)
    pl.semaphore_wait(barrier, SEQ - 1 + NX - 1)
    forward.share()

    flip_rows = (orders[0] + orders[1]) % 2
    flip_columns = (orders[0] // 2 + orders[1] // 2 + s) % 2
    row = iota((4 * T, T), 0)
    device, quarter, line = row // 16, (row // 4) % 4, row % 4
    token = line * SEQ + jnp.where((line + flip_rows) % 2 == 0, device, SEQ - 1 - device)
    column = iota((4 * T, T), 1)
    end(loads[3:4])
    packed = jnp.zeros((4 * T, T), F32)
    for j in range(4):
        pick = jnp.where((token == column) & (quarter == j), 1.0, 0.0).astype(BF16)
        packed = packed + mm(pick, ref.og[:, 256 * j : 256 * j + 256])
    ref.swap_out[...] = packed.astype(BF16).reshape(SEQ, 16, 256)

    forward.send()

    def swap(i):
        to = (s + i) % SEQ
        return copy_to(ref.swap_out.at[to], ref.swap_in.at[s], ref.swap_s.at[i], ref.swap_r.at[i], to, x)

    each(SEQ, lambda i: swap(i).start())
    ref.swap_in[pl.ds(s, 1)] = ref.swap_out[pl.ds(s, 1)]

    lower = iota((T, T), 0) >= iota((T, T), 1)
    ref.mixing[...] = jnp.where(lower, mm(c, b, 1, 1), 0.0)
    ref.inner[...] = mm_split(ref.mixing[...], ref.pushed[...])
    ref.up[...] = expand(ref.u[...])
    ref.skip[...] = expand(jnp.broadcast_to(skip_ref[...], (8, HEADS)))
    forward.fold()
    end(loads[4:5])
    gate = ref.z[...].astype(F32)
    sigma = jax.nn.sigmoid(gate)
    ref.active[...] = gate * sigma
    ref.slope[...] = sigma * (1.0 + gate * (1.0 - sigma))
    forward.answer()
    forward.halve()

    each(SEQ, lambda i: swap(i).wait())
    arrived = ref.swap_in[...].reshape(4 * T, 256)
    at = iota((T, 4 * T), 0)
    source = jnp.where(flip_columns == 0, at, T - 1 - at)
    source = (source // 4) * 16 + source % 4
    column = iota((T, 4 * T), 1)
    for j in range(4):
        pick = jnp.where(source + 4 * j == column, 1.0, 0.0).astype(BF16)
        ref.grads[:, 256 * j : 256 * j + 256] = mm(pick, arrived).astype(BF16)
    share_grads = copy_to(ref.grads, ref.peer_grads, ref.pair_s.at[0], ref.pair_r.at[0], other, x)
    share_grads.start()

    forward.finish(ref.entering, ref.half[0:1])
    gain = gain_ref[...]
    mixed = ref.up[...] * (ref.inner[...] + mm_exact_left(c, ref.entering[...]))
    mixed = mixed + ref.skip[0:1] * ref.x[...].astype(F32)
    ref.inner[...] = mixed
    gated = mixed * ref.active[...]
    inverse = lax.rsqrt(jnp.mean(gated * gated, axis=1, keepdims=True) + EPSILON)
    ref.inverse[...] = inverse
    unit = gated * inverse
    ref.unit[...] = unit
    ref.normed[...] = (unit * gain).astype(BF16)

    share_normed = copy_to(
        ref.normed.at[:, rows(1 - core, 512)], ref.peer_normed, ref.pair_s.at[1], ref.pair_r.at[1], other, x
    )
    share_normed.start()
    ref.mine[...] = mm(ref.normed[:, rows(core, 512)], ref.grads[...], 0, 0)
    end([share_grads, share_normed])
    ref.mine[...] += mm(ref.peer_normed[...], ref.peer_grads[...], 0, 0)
    ref.rough[...] = ref.mine[...].astype(BF16)

    def along_x(i):
        return s, (x + i) % NX

    def along_y(i):
        return ((y + i) % NY) * GROUP + m, x

    def along_z(i):
        return y * GROUP + ((z + i) % NZ) * 2 + core, x

    def to_each(count, send, recv, peer, src, dst):
        return [copy_to(src(i), dst(i), send.at[i], recv.at[i], *peer(i)) for i in far_first(count)]

    left, right = slice(0, 512), slice(512, 1024)
    ring_a, ring_b = Ring(ring_a, x, along_x), Ring(ring_b, y, along_y)
    ring_a.start_sum(ref.rough, left)
    ring_b.start_sum(ref.rough, right)

    end(loads[5:6])
    d_normed = mm(ref.grads[...], ref.w[...], 1, 1)
    ref.d_normed[...] = d_normed
    unit = ref.unit[...]
    scaled = d_normed * gain
    d_gated = ref.inverse[...] * (scaled - unit * jnp.mean(scaled * unit, axis=1, keepdims=True))
    d_mixed = d_gated * ref.active[...]
    ref.d_mixed[...] = d_mixed
    ref.pulled[...] = ref.up[...] * d_mixed
    backward = StateExchange(ref_b, BACKWARD[0], True)
    half = ref.half[...]
    backward.start(half[0:1] * mm_exact_left(c, ref.pulled[...], 0, 0), half * half)
    backward.share()
    ring_a.pass_sum(ref.mine, left)
    ring_b.pass_sum(ref.mine, right)
    gain_sum = jnp.sum(ref.d_normed[...] * ref.unit[...], axis=0, keepdims=True)
    skip_sum = jnp.sum(ref.d_mixed[...] * ref.x[...].astype(F32), axis=0, keepdims=True)
    for k in range(8):
        lanes = slice(128 * k, 128 * k + 128)
        rounds[0].mine[k : k + 1] = gain_sum[:, lanes]
        rounds[0].mine[8 + k : 9 + k] = skip_sum[:, lanes]

    def sum_round(one, count, peer):
        return to_each(count, one.s, one.r, peer, lambda i: one.mine, lambda i: one.theirs.at[i - 1])

    def sum_end(one, copies):
        end(copies)
        total = one.mine[...]
        for i in range(len(copies)):
            total = total + one.theirs[i]
        return total

    sums = sum_round(rounds[0], 2, lambda i: (other, x))
    begin(sums)
    backward.send()
    saves = []

    def save(src, dst):
        saves.append(pltpu.make_async_copy(src, dst, ref.save.at[len(saves)]))
        saves[-1].start()

    d_gated = ref.inverse[...] * (
        ref.d_normed[...] * gain - ref.unit[...] * jnp.mean(ref.d_normed[...] * gain * ref.unit[...], axis=1, keepdims=True)
    )
    ref.gate_grad[...] = (d_gated * ref.inner[...] * ref.slope[...]).astype(BF16)
    save(ref.gate_grad, gate_grad_out)

    ref.a1[...] = ring_a.end_sum(ref.mine, left)
    ref.b1[...] = ring_b.end_sum(ref.mine, right)
    ref.a1_out[...] = ref.a1[...].astype(BF16)
    ref.b1_out[...] = ref.b1[...].astype(BF16)
    second = to_each(
        NY, ref.a2_s, ref.a2_r, along_y, lambda i: ref.a1_out.at[rows((y + i) % NY, 32)], lambda i: ref.a2.at[i - 1]
    ) + to_each(
        NX, ref.b2_s, ref.b2_r, along_x, lambda i: ref.b1_out.at[rows((x + i) % NX, 32)], lambda i: ref.b2.at[i - 1]
    )
    begin(second)
    backward.fold()
    rounds[1].mine[...] = sum_end(rounds[0], sums)
    sums = sum_round(rounds[1], NX, along_x)
    begin(sums)

    end(second)
    a2 = ref.a1[rows(y, 32), :] + (ref.a2[0].astype(F32) + ref.a2[1].astype(F32) + ref.a2[2].astype(F32))
    b2 = ref.b1[rows(x, 32), :] + (ref.b2[0].astype(F32) + ref.b2[1].astype(F32) + ref.b2[2].astype(F32))
    for k in range(4):
        part = (slice(16 * (k // 2), 16 * (k // 2) + 16), slice(256 * (k % 2), 256 * (k % 2) + 256))
        ref.c1[k] = a2[part]
        ref.c1[k + 4] = b2[part]
    third = to_each(
        NZ, ref.c3_s, ref.c3_r, along_z, lambda i: ref.c1.at[(z + i) % NZ], lambda i: ref.c3.at[i - 1]
    )
    begin(third)
    backward.answer()
    rounds[2].mine[...] = sum_end(rounds[1], sums)
    sums = sum_round(rounds[2], NY, along_y)
    begin(sums)
    pulled, pushed = ref.pulled[...], ref.pushed[...]
    paired = jnp.where(lower, mm_split(pulled, pushed, 1, 1), 0.0)
    ref.d_b[...] = mm_exact_right(paired, c, 0, 0)
    d_c = mm_exact_right(paired, b) + mm_split(pulled, ref.entering[...], 1, 1)
    ref.pair_grad[:, STATE : 2 * STATE] = d_c.astype(BF16)

    end(third)
    block = ref.c1[pl.ds(z, 1)][0]
    for i in range(NZ - 1):
        block = block + ref.c3[i]
    ref.c4[pl.ds(z, 1)] = block.astype(BF16)[None]
    mine = ref.c4.at[z]
    fourth = to_each(NZ, ref.c4_s, ref.c4_r, along_z, lambda i: mine, lambda i: mine)
    begin(fourth)
    backward.halve()
    rounds[3].mine[...] = sum_end(rounds[2], sums)
    sums = sum_round(rounds[3], NZ, along_z)
    begin(sums)
    ref.d_x[...] = mm_split(ref.mixing[...], ref.pulled[...], 0, 0)

    end(fourth)
    full, base = ref.full, core * 512
    for k in range(4):
        lanes = slice(256 * (k % 2), 256 * (k % 2) + 256)
        full[rows(k // 2, 16, base + 128 * x + 32 * y), lanes] = ref.c4[k]
        lanes = slice(512 + 256 * (k % 2), 512 + 256 * (k % 2) + 256)
        full[rows(k // 2, 16, base + 128 * y + 32 * x), lanes] = ref.c4[k + 4]
    at_a = full.at[rows(y, 32, base + 128 * x), left]
    at_b = full.at[rows(x, 32, base + 128 * y), right]
    fifth = to_each(NY, ref.a5_s, ref.a5_r, along_y, lambda i: at_a, lambda i: at_a) + to_each(
        NX, ref.b5_s, ref.b5_r, along_x, lambda i: at_b, lambda i: at_b
    )
    begin(fifth)
    backward.finish(ref.leaving, ref.half[0:1])
    end(fifth)
    ring_a.start_gather(full, base, left)
    ring_b.start_gather(full, base, right)

    last, others = [], []

    def hand_over(index, lanes):
        k, at = len(last), full.at[rows(index % 4, 128, base), lanes]
        last.append(copy_to(at, at, ref.last_s.at[k], ref.last_r.at[k], other, x))
        last[-1].start()
        save(at, full_out.at[rows(index % 4, 128, base), lanes])
        others.append((rows(index % 4, 128, 512 - base), lanes))

    hand_over(x, left)
    hand_over(y, right)
    leaving = ref.leaving[...]
    ref.pair_grad[:, 0:STATE] = (ref.d_b[...] + mm_split(ref.pushed[...], leaving, 1, 1)).astype(BF16)
    save(ref.pair_grad, pair_grad_out)
    ring_a.pass_gather()
    ring_b.pass_gather()
    ref.input_grad[...] = (
        ref.down[...] * (ref.d_x[...] + mm_exact_left(b, leaving)) + ref.skip[0:1] * ref.d_mixed[...]
    ).astype(BF16)
    save(ref.input_grad, input_grad_out)
    end([ring_a.gathers[2]])
    hand_over(x + 3, left)
    end([ring_b.gathers[2]])
    hand_over(y + 3, right)
    end([ring_a.gathers[3]])
    hand_over(x + 1, left)
    end([ring_b.gathers[3]])
    hand_over(y + 1, right)
    ref.sums[...] = sum_end(rounds[3], sums)
    save(ref.sums, total_out)
    end(ring_a.gathers[4:6])
    hand_over(x + 2, left)
    end(ring_b.gathers[4:6])
    hand_over(y + 2, right)
    for one, at in zip(last, others):
        one.wait()
        save(full.at[at], full_out.at[at])
    end(saves)


PARTS = 8


def widen(
    total, full_in, input_grad_in, gate_grad_in, pair_grad_in,
    full_out, gain, skip, input_grad_out, gate_grad_out, pair_grad_out,
    narrow, wide, token_a, token_b, pair, loads, saves, moves, moved_on,
):
    moved = ((input_grad_in, token_a, input_grad_out), (gate_grad_in, token_b, gate_grad_out), (pair_grad_in, pair, pair_grad_out))
    fetch = [pltpu.make_async_copy(src, via, moves.at[k]) for k, (src, via, _) in enumerate(moved)]
    store = [pltpu.make_async_copy(via, dst, moved_on.at[k]) for k, (_, via, dst) in enumerate(moved)]
    size = W // PARTS
    at = [pl.ds(size * k, size) for k in range(PARTS)]
    loaded = [pltpu.make_async_copy(full_in.at[at[k]], narrow.at[at[k]], loads.at[k]) for k in range(PARTS)]
    saved = [pltpu.make_async_copy(wide.at[at[k]], full_out.at[at[k]], saves.at[k]) for k in range(PARTS)]
    begin(loaded)
    begin(fetch)
    for k in range(8):
        gain[0:1, 128 * k : 128 * k + 128] = total[k : k + 1]
    lane, head = iota((8, 128), 1), iota((8, HEADS), 1)
    first = jnp.sum(jnp.where(lane < 64, total[8:16], 0.0), axis=1, keepdims=True)
    second = jnp.sum(jnp.where(lane < 64, 0.0, total[8:16]), axis=1, keepdims=True)
    both = jnp.where(head % 2 == 0, first, second)
    skip[...] = jnp.sum(jnp.where(head // 2 == iota((8, HEADS), 0), both, 0.0), axis=0, keepdims=True)
    for k in range(PARTS):
        loaded[k].wait()
        wide[at[k], :] = narrow[at[k], :].astype(F32)
        saved[k].start()
    for one, two in zip(fetch, store):
        one.wait()
        two.start()
    end(saved)
    end(store)


ANY = pl.BlockSpec(memory_space=pl.ANY)
VM = pl.BlockSpec(memory_space=pltpu.VMEM)
SM = pl.BlockSpec(memory_space=pltpu.SMEM)


def local(inputs, gates, pairs, steps, log_decay, skip, gain, out_weight, out_grad, order_ids):
    token, pair = jax.ShapeDtypeStruct((T, W), BF16), jax.ShapeDtypeStruct((T, 2 * STATE), BF16)
    input_grad, gate_grad, pair_grad, full, total = pl.pallas_call(
        kernel,
        out_shape=[token, token, pair, jax.ShapeDtypeStruct((W, W), BF16), jax.ShapeDtypeStruct((16, 128), F32)],
        in_specs=[SM, VM, VM, VM] + [ANY] * 6,
        out_specs=[ANY] * 5,
        scratch_shapes=[one for group in BUFFERS for one in group.values()],
        compiler_params=pltpu.CompilerParams(vmem_limit_bytes=VMEM_LIMIT, collective_id=0, has_side_effects=True),
    )(
        order_ids, log_decay[None], skip[None], gain[None], inputs[0], gates[0], pairs[0], steps[0], out_weight, out_grad[0]
    )

    weight_grad, gain_grad, skip_grad, input_grad, gate_grad, pair_grad = pl.pallas_call(
        widen,
        out_shape=[
            jax.ShapeDtypeStruct((W, W), F32),
            jax.ShapeDtypeStruct((1, W), F32),
            jax.ShapeDtypeStruct((1, HEADS), F32),
            token,
            token,
            pair,
        ],
        in_specs=[VM] + [ANY] * 4,
        out_specs=[ANY, VM, VM, ANY, ANY, ANY],
        scratch_shapes=[
            pltpu.VMEM((W, W), BF16), pltpu.VMEM((W, W), F32), pltpu.VMEM((T, W), BF16), pltpu.VMEM((T, W), BF16),
            pltpu.VMEM((T, 2 * STATE), BF16), dma(PARTS), dma(PARTS), dma(3), dma(3),
        ],
        compiler_params=pltpu.CompilerParams(vmem_limit_bytes=VMEM_LIMIT),
    )(total, full, input_grad, gate_grad, pair_grad)
    return input_grad[None], gate_grad[None], pair_grad[None], weight_grad, gain_grad[0], skip_grad[0]


def solution(mesh):
    token = P("dp", "seq", None)
    return jax.shard_map(
        local,
        mesh=mesh,
        in_specs=(token, token, token, P("dp", None, "seq"), P(), P(), P(), P(), token, P()),
        out_specs=(token, token, token, P(), P(), P()),
        check_vma=False,
    )
```

time: 899 us -> 85.2 us (0.09)
  blocking collectives: 331 us -> 0 us
  other arithmetic: 230 us -> 0 us
  waiting for transfers between devices: 173 us -> 0 us
  local copies, waits for them, and re-layouts: 90.7 us -> 0 us
  Pallas kernels: 0 us -> 84.3 us
  matrix products: 30.1 us -> 0 us
  between operations: 20.4 us -> 0.8 us
  starting transfers between devices: 13.7 us -> 0 us
    unnamed x2 -> x0, blocking collectives: 258 us -> none
    select_n x131 -> x0, other arithmetic: 212 us -> none  [the longest x128 211 us: step(): return jax.tree.map(lambda a, b: jnp.where(reached, a, b), new, before)]
    psum x1 -> x0, waiting for transfers between devices: 173 us -> none  [local(): lax.psum((weight_term, gain_part, skip_part), ('seq', 'dp'))]
    pallas_call x0 -> x2, Pallas kernels: none -> 84.3 us  [the longest x1 79.5 us: local(): pl.pallas_call(kernel, out_shape=[token, token, pair, jax.ShapeDtypeStruc...]
    psum x1 -> x0, blocking collectives: 73.7 us -> none  [local(): lax.psum((weight_term, gain_part, skip_part), ('seq', 'dp'))]
    mul x130 -> x0, local copies, waits for them, and re-layouts: 45.3 us -> none  [the longest x128 44.9 us: combine_states(): later[0][:, None, None] * earlier[1] + later[1]]
    dot_general x14 -> x0, matrix products: 30.1 us -> none  [the longest x1 5.14 us: local(): jnp.einsum('chi,chpn,cin->cihp', growth, starts, input_c_matrix, precisio...]
    all_to_all x1 -> x0, starting transfers between devices: 13.3 us -> none  [local(): lax.all_to_all(outgoing, 'seq', split_axis=1, concat_axis=2, tiled=True)]
  transfers between devices with their start and end apart: 4 -> 0, of which waited for: 1 -> 0; matrix products, arithmetic and copies ran while one was open for 14% -> 0% of each run, Pallas kernels for 0% -> 0%
where the time goes in v2:
time: 85.2 us; the launch traced here: 85.1 us
  Pallas kernels  84.3 us (99%)
    pallas_call x1, Pallas kernels, local(): pl.pallas_call(kernel, out_shape=[token, token, pair, jax.ShapeDtypeStruc...  79.5 us
    pallas_call x1, Pallas kernels, local(): pl.pallas_call(widen, out_shape=[jax.ShapeDtypeStruct((W, W), F32), jax.S...  4.81 us

profile of v2, /device:TPU:1, one launch (start us, length us, event | category | flops | bytes accessed | tf_op | source)
XLA Modules:
  0.0 85.1 jit_solution(12899684445536791721)
XLA Ops:
  0.6 79.5 %shard_map.145 = (bf16[256,1024]{1,0:T(8,128)(2,1)}, bf16[256,1024]{1,0:T(8,128)(2,1)}, bf16[256,128]{1,0:T(8,128)(2,1)}, bf16[1024,1024]{1,0:T(8,128)(2,1)}, f32[16,128]{1,0:T(8,128)}) custom-call(s32[2]{0:T(128)} %orders.1, f32[1,16]{1,0:T(1,128)} %bitcast.19, f32[1,16]{1,0:T(1,128)} %bitcast.20, f32[1,1024]{1,0:T(1,128)} %bitcast.18, ...), custom_call_target="tpu_custom_call" | custom-call | tf_op jit(solution)/shard_map/pallas_call | solution.py:716
  80.1 4.8 %shard_map.146 = (f32[1024,1024]{1,0:T(8,128)}, f32[1,1024]{1,0:T(1,128)}, f32[1,16]{1,0:T(1,128)}, bf16[256,1024]{1,0:T(8,128)(2,1)}, bf16[256,1024]{1,0:T(8,128)(2,1)}, /*index=5*/bf16[256,128]{1,0:T(8,128)(2,1)}) custom-call(f32[16,128]{1,0:T(8,128)} %get-tuple-element.17.total, bf16[1024,1024]{1,0:T(8,128)(2,1)} %get-tuple-element.18.full_in, ...), custom_call_target="tpu_custom_call" | custom-call | tf_op jit(solution)/shard_map/pallas_call | solution.py:727

commit v3 on v2

--- a/solution.py
+++ b/solution.py
@@ -331,8 +331,8 @@
         bc=pltpu.VMEM((T, 2 * STATE), BF16),
         dt=pltpu.VMEM((HEADS, T), F32),
         w=pltpu.VMEM((W, W), BF16),
+        entered=pltpu.SemaphoreType.REGULAR,
         load=dma(6),
-        save=dma(20),
         swap_out=pltpu.VMEM((SEQ, 16, 256), BF16),
         swap_in=pltpu.VMEM((SEQ, 16, 256), BF16),
         swap_s=dma(SEQ),
@@ -358,9 +358,6 @@
         pulled=full,
         d_x=full,
         d_b=pltpu.VMEM((T, STATE), F32),
-        gate_grad=half,
-        input_grad=half,
-        pair_grad=pltpu.VMEM((T, 2 * STATE), BF16),
         peer_normed=pltpu.VMEM((T, 512), BF16),
         peer_grads=half,
         pair_s=dma(2),
@@ -379,9 +376,7 @@
         c3_s=dma(8), c3_r=dma(8), c4_s=dma(8), c4_r=dma(8),
         c4=pltpu.VMEM((8, 16, 256), BF16),
         a5_s=dma(4), a5_r=dma(4), b5_s=dma(4), b5_r=dma(4),
-        full=pltpu.VMEM((W, W), BF16),
         last_s=dma(8), last_r=dma(8),
-        sums=pltpu.VMEM((16, 128), F32),
     )
     rounds = [
         dict(
@@ -398,7 +393,7 @@
 
 def kernel(
     orders, decay_ref, skip_ref, gain_ref, x_in, z_in, bc_in, dt_in, w_in, og_in,
-    input_grad_out, gate_grad_out, pair_grad_out, full_out, total_out, *scratch,
+    input_grad, gate_grad, pair_grad, full, total, *scratch,
 ):
     scratch = iter(scratch)
     ref, ref_f, ref_b, ring_a, ring_b, *rounds = [
@@ -416,8 +411,12 @@
     operands = ((dt_in, ref.dt), (bc_in, ref.bc), (x_in, ref.x), (og_in, ref.og), (z_in, ref.z), (w_in, ref.w))
     loads = [pltpu.make_async_copy(src, dst, ref.load.at[k]) for k, (src, dst) in enumerate(operands)]
     begin(loads)
-    each(SEQ, lambda i: hello((s + i) % SEQ, x))
-    each(NX, lambda i: hello(s, (x + i) % NX))
+    for i in far_first(GROUP):
+        hello(y * GROUP + (m + i) % GROUP, x)
+    for i in far_first(NY):
+        hello(((y + i) % NY) * GROUP + m, x)
+    for i in far_first(NX):
+        hello(s, (x + i) % NX)
 
     end(loads[0:1])
     ref.u[...], down, half = scales(ref.dt[...], decay_ref[...])
@@ -427,7 +426,11 @@
     forward = StateExchange(ref_f, FORWARD[0], False)
     b, c = ref.bc[:, 0:STATE], ref.bc[:, STATE : 2 * STATE]
     forward.start(half[0:1] * mm_exact_left(b, ref.pushed[...], 0, 0), half * half)
-    pl.semaphore_wait(barrier, SEQ - 1 + NX - 1)
+    pl.semaphore_wait(barrier, GROUP - 1 + NY - 1 + NX - 1)
+    for i in far_first(NY):
+        pl.semaphore_signal(
+            ref.entered, inc=1, device_id=dict(seq=((y + i) % NY) * GROUP + m, dp=x), device_id_type=MESH
+        )
     forward.share()
 
     flip_rows = (orders[0] + orders[1]) % 2
@@ -444,6 +447,8 @@
     ref.swap_out[...] = packed.astype(BF16).reshape(SEQ, 16, 256)
 
     forward.send()
+
+    pl.semaphore_wait(ref.entered, NY - 1)
 
     def swap(i):
         to = (s + i) % SEQ
@@ -551,17 +556,11 @@
     sums = sum_round(rounds[0], 2, lambda i: (other, x))
     begin(sums)
     backward.send()
-    saves = []
-
-    def save(src, dst):
-        saves.append(pltpu.make_async_copy(src, dst, ref.save.at[len(saves)]))
-        saves[-1].start()
 
     d_gated = ref.inverse[...] * (
         ref.d_normed[...] * gain - ref.unit[...] * jnp.mean(ref.d_normed[...] * gain * ref.unit[...], axis=1, keepdims=True)
     )
-    ref.gate_grad[...] = (d_gated * ref.inner[...] * ref.slope[...]).astype(BF16)
-    save(ref.gate_grad, gate_grad_out)
+    gate_grad[...] = (d_gated * ref.inner[...] * ref.slope[...]).astype(BF16)
 
     ref.a1[...] = ring_a.end_sum(ref.mine, left)
     ref.b1[...] = ring_b.end_sum(ref.mine, right)
@@ -597,7 +596,7 @@
     paired = jnp.where(lower, mm_split(pulled, pushed, 1, 1), 0.0)
     ref.d_b[...] = mm_exact_right(paired, c, 0, 0)
     d_c = mm_exact_right(paired, b) + mm_split(pulled, ref.entering[...], 1, 1)
-    ref.pair_grad[:, STATE : 2 * STATE] = d_c.astype(BF16)
+    pair_grad[:, STATE : 2 * STATE] = d_c.astype(BF16)
 
     end(third)
     block = ref.c1[pl.ds(z, 1)][0]
@@ -614,7 +613,7 @@
     ref.d_x[...] = mm_split(ref.mixing[...], ref.pulled[...], 0, 0)
 
     end(fourth)
-    full, base = ref.full, core * 512
+    base = core * 512
     for k in range(4):
         lanes = slice(256 * (k % 2), 256 * (k % 2) + 256)
         full[rows(k // 2, 16, base + 128 * x + 32 * y), lanes] = ref.c4[k]
@@ -631,26 +630,22 @@
     ring_a.start_gather(full, base, left)
     ring_b.start_gather(full, base, right)
 
-    last, others = [], []
+    last = []
 
     def hand_over(index, lanes):
         k, at = len(last), full.at[rows(index % 4, 128, base), lanes]
         last.append(copy_to(at, at, ref.last_s.at[k], ref.last_r.at[k], other, x))
         last[-1].start()
-        save(at, full_out.at[rows(index % 4, 128, base), lanes])
-        others.append((rows(index % 4, 128, 512 - base), lanes))
 
     hand_over(x, left)
     hand_over(y, right)
     leaving = ref.leaving[...]
-    ref.pair_grad[:, 0:STATE] = (ref.d_b[...] + mm_split(ref.pushed[...], leaving, 1, 1)).astype(BF16)
-    save(ref.pair_grad, pair_grad_out)
+    pair_grad[:, 0:STATE] = (ref.d_b[...] + mm_split(ref.pushed[...], leaving, 1, 1)).astype(BF16)
     ring_a.pass_gather()
     ring_b.pass_gather()
-    ref.input_grad[...] = (
+    input_grad[...] = (
         ref.down[...] * (ref.d_x[...] + mm_exact_left(b, leaving)) + ref.skip[0:1] * ref.d_mixed[...]
     ).astype(BF16)
-    save(ref.input_grad, input_grad_out)
     end([ring_a.gathers[2]])
     hand_over(x + 3, left)
     end([ring_b.gathers[2]])
@@ -659,16 +654,12 @@
     hand_over(x + 1, left)
     end([ring_b.gathers[3]])
     hand_over(y + 1, right)
-    ref.sums[...] = sum_end(rounds[3], sums)
-    save(ref.sums, total_out)
+    total[...] = sum_end(rounds[3], sums)
     end(ring_a.gathers[4:6])
     hand_over(x + 2, left)
     end(ring_b.gathers[4:6])
     hand_over(y + 2, right)
-    for one, at in zip(last, others):
-        one.wait()
-        save(full.at[at], full_out.at[at])
-    end(saves)
+    end(last)
 
 
 PARTS = 8
@@ -677,17 +668,18 @@
 def widen(
     total, full_in, input_grad_in, gate_grad_in, pair_grad_in,
     full_out, gain, skip, input_grad_out, gate_grad_out, pair_grad_out,
-    narrow, wide, token_a, token_b, pair, loads, saves, moves, moved_on,
+    wide, saves, moves,
 ):
-    moved = ((input_grad_in, token_a, input_grad_out), (gate_grad_in, token_b, gate_grad_out), (pair_grad_in, pair, pair_grad_out))
-    fetch = [pltpu.make_async_copy(src, via, moves.at[k]) for k, (src, via, _) in enumerate(moved)]
-    store = [pltpu.make_async_copy(via, dst, moved_on.at[k]) for k, (_, via, dst) in enumerate(moved)]
+    moved = ((input_grad_in, input_grad_out), (gate_grad_in, gate_grad_out), (pair_grad_in, pair_grad_out))
+    store = [pltpu.make_async_copy(src, dst, moves.at[k]) for k, (src, dst) in enumerate(moved)]
+    begin(store)
     size = W // PARTS
-    at = [pl.ds(size * k, size) for k in range(PARTS)]
-    loaded = [pltpu.make_async_copy(full_in.at[at[k]], narrow.at[at[k]], loads.at[k]) for k in range(PARTS)]
-    saved = [pltpu.make_async_copy(wide.at[at[k]], full_out.at[at[k]], saves.at[k]) for k in range(PARTS)]
-    begin(loaded)
-    begin(fetch)
+    saved = []
+    for k in range(PARTS):
+        at = pl.ds(size * k, size)
+        wide[at, :] = full_in[at, :].astype(F32)
+        saved.append(pltpu.make_async_copy(wide.at[at], full_out.at[at], saves.at[k]))
+        saved[k].start()
     for k in range(8):
         gain[0:1, 128 * k : 128 * k + 128] = total[k : k + 1]
     lane, head = iota((8, 128), 1), iota((8, HEADS), 1)
@@ -695,13 +687,6 @@
     second = jnp.sum(jnp.where(lane < 64, 0.0, total[8:16]), axis=1, keepdims=True)
     both = jnp.where(head % 2 == 0, first, second)
     skip[...] = jnp.sum(jnp.where(head // 2 == iota((8, HEADS), 0), both, 0.0), axis=0, keepdims=True)
-    for k in range(PARTS):
-        loaded[k].wait()
-        wide[at[k], :] = narrow[at[k], :].astype(F32)
-        saved[k].start()
-    for one, two in zip(fetch, store):
-        one.wait()
-        two.start()
     end(saved)
     end(store)
 
@@ -712,12 +697,12 @@
 
 
 def local(inputs, gates, pairs, steps, log_decay, skip, gain, out_weight, out_grad, order_ids):
-    token, pair = jax.ShapeDtypeStruct((T, W), BF16), jax.ShapeDtypeStruct((T, 2 * STATE), BF16)
+    token, pair = ((T, W), BF16), ((T, 2 * STATE), BF16)
     input_grad, gate_grad, pair_grad, full, total = pl.pallas_call(
         kernel,
-        out_shape=[token, token, pair, jax.ShapeDtypeStruct((W, W), BF16), jax.ShapeDtypeStruct((16, 128), F32)],
+        out_shape=[pltpu.VMEM(*one) for one in (token, token, pair, ((W, W), BF16), ((16, 128), F32))],
         in_specs=[SM, VM, VM, VM] + [ANY] * 6,
-        out_specs=[ANY] * 5,
+        out_specs=[VM] * 5,
         scratch_shapes=[one for group in BUFFERS for one in group.values()],
         compiler_params=pltpu.CompilerParams(vmem_limit_bytes=VMEM_LIMIT, collective_id=0, has_side_effects=True),
     )(
@@ -727,20 +712,12 @@
     weight_grad, gain_grad, skip_grad, input_grad, gate_grad, pair_grad = pl.pallas_call(
         widen,
         out_shape=[
-            jax.ShapeDtypeStruct((W, W), F32),
-            jax.ShapeDtypeStruct((1, W), F32),
-            jax.ShapeDtypeStruct((1, HEADS), F32),
-            token,
-            token,
-            pair,
+            jax.ShapeDtypeStruct(*one) for one in (((W, W), F32), ((1, W), F32), ((1, HEADS), F32), token, token, pair)
         ],
-        in_specs=[VM] + [ANY] * 4,
+        in_specs=[VM] * 5,
         out_specs=[ANY, VM, VM, ANY, ANY, ANY],
-        scratch_shapes=[
-            pltpu.VMEM((W, W), BF16), pltpu.VMEM((W, W), F32), pltpu.VMEM((T, W), BF16), pltpu.VMEM((T, W), BF16),
-            pltpu.VMEM((T, 2 * STATE), BF16), dma(PARTS), dma(PARTS), dma(3), dma(3),
-        ],
-        compiler_params=pltpu.CompilerParams(vmem_limit_bytes=VMEM_LIMIT),
+        scratch_shapes=[pltpu.VMEM((W, W), F32), dma(PARTS), dma(3)],
+        compiler_params=pltpu.CompilerParams(vmem_limit_bytes=16 * 1024 * 1024),
     )(total, full, input_grad, gate_grad, pair_grad)
     return input_grad[None], gate_grad[None], pair_grad[None], weight_grad, gain_grad[0], skip_grad[0]
 

time: 85.2 us -> 80.9 us (0.950)
  Pallas kernels: 84.3 us -> 79.9 us
    pallas_call x2, Pallas kernels: 84.3 us -> 79.9 us  [the longest x1 76.9 us: local(): pl.pallas_call(kernel, out_shape=[pltpu.VMEM(*one) for one in (token, tok...]
where the time goes in v3:
time: 80.9 us; the launch traced here: 80.7 us
  Pallas kernels  79.9 us (99%)
    pallas_call x1, Pallas kernels, local(): pl.pallas_call(kernel, out_shape=[pltpu.VMEM(*one) for one in (token, tok...  76.9 us
    pallas_call x1, Pallas kernels, local(): pl.pallas_call(widen, out_shape=[jax.ShapeDtypeStruct(*one) for one in ((...  3.05 us

profile of v3, /device:TPU:1, one launch (start us, length us, event | category | flops | bytes accessed | tf_op | source)
XLA Modules:
  0.0 80.7 jit_solution(9611719552167053916)
XLA Ops:
  0.6 76.9 %shard_map.145 = (bf16[256,1024]{1,0:T(8,128)(2,1)S(1)}, bf16[256,1024]{1,0:T(8,128)(2,1)S(1)}, bf16[256,128]{1,0:T(8,128)(2,1)S(1)}, bf16[1024,1024]{1,0:T(8,128)(2,1)S(1)}, f32[16,128]{1,0:T(8,128)S(1)}) custom-call(s32[2]{0:T(128)} %orders.1, f32[1,16]{1,0:T(1,128)} %bitcast.19, f32[1,16]{1,0:T(1,128)} %bitcast.20, f32[1,1024]{1,0:T(1,128)} %bitcast.18, ...), custom_call_target="tpu_custom_call" | custom-call | tf_op jit(solution)/shard_map/pallas_call | solution.py:701
  77.5 3.0 %shard_map.146 = (f32[1024,1024]{1,0:T(8,128)}, f32[1,1024]{1,0:T(1,128)}, f32[1,16]{1,0:T(1,128)}, bf16[256,1024]{1,0:T(8,128)(2,1)}, bf16[256,1024]{1,0:T(8,128)(2,1)}, /*index=5*/bf16[256,128]{1,0:T(8,128)(2,1)}) custom-call(f32[16,128]{1,0:T(8,128)S(1)} %get-tuple-element.17.total, bf16[1024,1024]{1,0:T(8,128)(2,1)S(1)} %get-tuple-element.18.full_in, ...), custom_call_target="tpu_custom_call" | custom-call | tf_op jit(solution)/shard_map/pallas_call | solution.py:712

commit v4 on v3

--- a/solution.py
+++ b/solution.py
@@ -372,10 +372,11 @@
         b2=pltpu.VMEM((3, 32, 512), BF16),
         a2_s=dma(4), a2_r=dma(4), b2_s=dma(4), b2_r=dma(4),
         c1=pltpu.VMEM((8, 16, 256), F32),
-        c3=pltpu.VMEM((7, 16, 256), F32),
+        c1_out=pltpu.VMEM((8, 16, 256), BF16),
+        c3=pltpu.VMEM((7, 16, 256), BF16),
         c3_s=dma(8), c3_r=dma(8), c4_s=dma(8), c4_r=dma(8),
         c4=pltpu.VMEM((8, 16, 256), BF16),
-        a5_s=dma(4), a5_r=dma(4), b5_s=dma(4), b5_r=dma(4),
+        c5_s=dma(8, 4), c5_r=dma(8, 4),
         last_s=dma(8), last_r=dma(8),
     )
     rounds = [
@@ -433,6 +434,8 @@
         )
     forward.share()
 
+    forward.send()
+
     flip_rows = (orders[0] + orders[1]) % 2
     flip_columns = (orders[0] // 2 + orders[1] // 2 + s) % 2
     row = iota((4 * T, T), 0)
@@ -445,8 +448,6 @@
         pick = jnp.where((token == column) & (quarter == j), 1.0, 0.0).astype(BF16)
         packed = packed + mm(pick, ref.og[:, 256 * j : 256 * j + 256])
     ref.swap_out[...] = packed.astype(BF16).reshape(SEQ, 16, 256)
-
-    forward.send()
 
     pl.semaphore_wait(ref.entered, NY - 1)
 
@@ -584,8 +585,9 @@
         part = (slice(16 * (k // 2), 16 * (k // 2) + 16), slice(256 * (k % 2), 256 * (k % 2) + 256))
         ref.c1[k] = a2[part]
         ref.c1[k + 4] = b2[part]
+    ref.c1_out[...] = ref.c1[...].astype(BF16)
     third = to_each(
-        NZ, ref.c3_s, ref.c3_r, along_z, lambda i: ref.c1.at[(z + i) % NZ], lambda i: ref.c3.at[i - 1]
+        NZ, ref.c3_s, ref.c3_r, along_z, lambda i: ref.c1_out.at[(z + i) % NZ], lambda i: ref.c3.at[i - 1]
     )
     begin(third)
     backward.answer()
@@ -601,31 +603,42 @@
     end(third)
     block = ref.c1[pl.ds(z, 1)][0]
     for i in range(NZ - 1):
-        block = block + ref.c3[i]
+        block = block + ref.c3[i].astype(F32)
     ref.c4[pl.ds(z, 1)] = block.astype(BF16)[None]
     mine = ref.c4.at[z]
-    fourth = to_each(NZ, ref.c4_s, ref.c4_r, along_z, lambda i: mine, lambda i: mine)
-    begin(fourth)
+    fourth = dict(zip(far_first(NZ), to_each(NZ, ref.c4_s, ref.c4_r, along_z, lambda i: mine, lambda i: mine)))
+    begin(fourth.values())
+
+    base, fifth = core * 512, []
+
+    def spread(j):
+        over_x = j // 4
+        outer, inner = x + over_x * (y - x), y + over_x * (x - y)
+        at = (
+            rows((j % 4) // 2, 16, base + 128 * outer + 32 * inner),
+            pl.ds(pl.multiple_of(512 * over_x + 256 * (j % 2), 256), 256),
+        )
+        for i in far_first(NX):
+            seq = s + (1 - over_x) * (((y + i) % NY) * GROUP + m - s)
+            dp = x + over_x * ((x + i) % NX - x)
+            fifth.append(copy_to(ref.c4.at[j], full.at[at], ref.c5_s.at[j, i], ref.c5_r.at[j, i], seq, dp))
+            fifth[-1].start()
+        full[at] = ref.c4[pl.ds(j, 1)][0]
+
+    spread(z)
     backward.halve()
     rounds[3].mine[...] = sum_end(rounds[2], sums)
     sums = sum_round(rounds[3], NZ, along_z)
     begin(sums)
+    for i in far_first(NZ)[::-1]:
+        fourth[i].wait()
+        spread((z + NZ - i) % NZ)
     ref.d_x[...] = mm_split(ref.mixing[...], ref.pulled[...], 0, 0)
-
-    end(fourth)
-    base = core * 512
-    for k in range(4):
-        lanes = slice(256 * (k % 2), 256 * (k % 2) + 256)
-        full[rows(k // 2, 16, base + 128 * x + 32 * y), lanes] = ref.c4[k]
-        lanes = slice(512 + 256 * (k % 2), 512 + 256 * (k % 2) + 256)
-        full[rows(k // 2, 16, base + 128 * y + 32 * x), lanes] = ref.c4[k + 4]
-    at_a = full.at[rows(y, 32, base + 128 * x), left]
-    at_b = full.at[rows(x, 32, base + 128 * y), right]
-    fifth = to_each(NY, ref.a5_s, ref.a5_r, along_y, lambda i: at_a, lambda i: at_a) + to_each(
-        NX, ref.b5_s, ref.b5_r, along_x, lambda i: at_b, lambda i: at_b
-    )
-    begin(fifth)
     backward.finish(ref.leaving, ref.half[0:1])
+    leaving = ref.leaving[...]
+    input_grad[...] = (
+        ref.down[...] * (ref.d_x[...] + mm_exact_left(b, leaving)) + ref.skip[0:1] * ref.d_mixed[...]
+    ).astype(BF16)
     end(fifth)
     ring_a.start_gather(full, base, left)
     ring_b.start_gather(full, base, right)
@@ -639,13 +652,8 @@
 
     hand_over(x, left)
     hand_over(y, right)
-    leaving = ref.leaving[...]
-    pair_grad[:, 0:STATE] = (ref.d_b[...] + mm_split(ref.pushed[...], leaving, 1, 1)).astype(BF16)
     ring_a.pass_gather()
     ring_b.pass_gather()
-    input_grad[...] = (
-        ref.down[...] * (ref.d_x[...] + mm_exact_left(b, leaving)) + ref.skip[0:1] * ref.d_mixed[...]
-    ).astype(BF16)
     end([ring_a.gathers[2]])
     hand_over(x + 3, left)
     end([ring_b.gathers[2]])
@@ -655,6 +663,7 @@
     end([ring_b.gathers[3]])
     hand_over(y + 1, right)
     total[...] = sum_end(rounds[3], sums)
+    pair_grad[:, 0:STATE] = (ref.d_b[...] + mm_split(ref.pushed[...], leaving, 1, 1)).astype(BF16)
     end(ring_a.gathers[4:6])
     hand_over(x + 2, left)
     end(ring_b.gathers[4:6])

time: 80.9 us -> 79.6 us (0.984)
  Pallas kernels: 79.9 us -> 78.6 us
    pallas_call x1, Pallas kernels: 76.9 us -> 75.6 us  [local(): pl.pallas_call(kernel, out_shape=[pltpu.VMEM(*one) for one in (token, tok...]
where the time goes in v4:
time: 79.6 us; the launch traced here: 79.4 us
  Pallas kernels  78.6 us (99%)
  between operations  0.8 us (1%)
    pallas_call x1, Pallas kernels, local(): pl.pallas_call(kernel, out_shape=[pltpu.VMEM(*one) for one in (token, tok...  75.6 us
    pallas_call x1, Pallas kernels, local(): pl.pallas_call(widen, out_shape=[jax.ShapeDtypeStruct(*one) for one in ((...  3.05 us

profile of v4, /device:TPU:1, one launch (start us, length us, event | category | flops | bytes accessed | tf_op | source)
XLA Modules:
  0.0 79.4 jit_solution(11243739821391802587)
XLA Ops:
  0.6 75.6 %shard_map.145 = (bf16[256,1024]{1,0:T(8,128)(2,1)S(1)}, bf16[256,1024]{1,0:T(8,128)(2,1)S(1)}, bf16[256,128]{1,0:T(8,128)(2,1)S(1)}, bf16[1024,1024]{1,0:T(8,128)(2,1)S(1)}, f32[16,128]{1,0:T(8,128)S(1)}) custom-call(s32[2]{0:T(128)} %orders.1, f32[1,16]{1,0:T(1,128)} %bitcast.19, f32[1,16]{1,0:T(1,128)} %bitcast.20, f32[1,1024]{1,0:T(1,128)} %bitcast.18, ...), custom_call_target="tpu_custom_call" | custom-call | tf_op jit(solution)/shard_map/pallas_call | solution.py:710
  76.2 3.0 %shard_map.146 = (f32[1024,1024]{1,0:T(8,128)}, f32[1,1024]{1,0:T(1,128)}, f32[1,16]{1,0:T(1,128)}, bf16[256,1024]{1,0:T(8,128)(2,1)}, bf16[256,1024]{1,0:T(8,128)(2,1)}, /*index=5*/bf16[256,128]{1,0:T(8,128)(2,1)}) custom-call(f32[16,128]{1,0:T(8,128)S(1)} %get-tuple-element.17.total, bf16[1024,1024]{1,0:T(8,128)(2,1)S(1)} %get-tuple-element.18.full_in, ...), custom_call_target="tpu_custom_call" | custom-call | tf_op jit(solution)/shard_map/pallas_call | solution.py:721

commit v5 on v4

--- a/solution.py
+++ b/solution.py
@@ -626,14 +626,14 @@
         full[at] = ref.c4[pl.ds(j, 1)][0]
 
     spread(z)
+    ref.d_x[...] = mm_split(ref.mixing[...], ref.pulled[...], 0, 0)
+    for i in far_first(NZ)[::-1]:
+        fourth[i].wait()
+        spread((z + NZ - i) % NZ)
     backward.halve()
     rounds[3].mine[...] = sum_end(rounds[2], sums)
     sums = sum_round(rounds[3], NZ, along_z)
     begin(sums)
-    for i in far_first(NZ)[::-1]:
-        fourth[i].wait()
-        spread((z + NZ - i) % NZ)
-    ref.d_x[...] = mm_split(ref.mixing[...], ref.pulled[...], 0, 0)
     backward.finish(ref.leaving, ref.half[0:1])
     leaving = ref.leaving[...]
     input_grad[...] = (

time: 79.6 us -> 79.9 us (level)
  no operation moved by 1% of the time
where the time goes in v5:
time: 79.9 us; the launch traced here: 79.7 us
  Pallas kernels  78.9 us (99%)
  between operations  0.8 us (1%)
    pallas_call x1, Pallas kernels, local(): pl.pallas_call(kernel, out_shape=[pltpu.VMEM(*one) for one in (token, tok...  75.9 us
    pallas_call x1, Pallas kernels, local(): pl.pallas_call(widen, out_shape=[jax.ShapeDtypeStruct(*one) for one in ((...  3.05 us

profile of v5, /device:TPU:1, one launch (start us, length us, event | category | flops | bytes accessed | tf_op | source)
XLA Modules:
  0.0 79.7 jit_solution(1653836059037166505)
XLA Ops:
  0.6 75.9 %shard_map.145 = (bf16[256,1024]{1,0:T(8,128)(2,1)S(1)}, bf16[256,1024]{1,0:T(8,128)(2,1)S(1)}, bf16[256,128]{1,0:T(8,128)(2,1)S(1)}, bf16[1024,1024]{1,0:T(8,128)(2,1)S(1)}, f32[16,128]{1,0:T(8,128)S(1)}) custom-call(s32[2]{0:T(128)} %orders.1, f32[1,16]{1,0:T(1,128)} %bitcast.19, f32[1,16]{1,0:T(1,128)} %bitcast.20, f32[1,1024]{1,0:T(1,128)} %bitcast.18, ...), custom_call_target="tpu_custom_call" | custom-call | tf_op jit(solution)/shard_map/pallas_call | solution.py:710
  76.5 3.0 %shard_map.146 = (f32[1024,1024]{1,0:T(8,128)}, f32[1,1024]{1,0:T(1,128)}, f32[1,16]{1,0:T(1,128)}, bf16[256,1024]{1,0:T(8,128)(2,1)}, bf16[256,1024]{1,0:T(8,128)(2,1)}, /*index=5*/bf16[256,128]{1,0:T(8,128)(2,1)}) custom-call(f32[16,128]{1,0:T(8,128)S(1)} %get-tuple-element.17.total, bf16[1024,1024]{1,0:T(8,128)(2,1)S(1)} %get-tuple-element.18.full_in, ...), custom_call_target="tpu_custom_call" | custom-call | tf_op jit(solution)/shard_map/pallas_call | solution.py:721
